TPU v7x, 128 devices: a whole 4x4x4 slice. The times are simulated.
128 devices in a mesh: replica: 8 (over x_lo, y), tensor: 16 (over z, x_hi, core).
Axes of the slice: x: 4 (x_hi: 2, x_lo: 2; x = x_hi * 2 + x_lo), y: 4, z: 4, core: 2. Of those that a mesh axis runs over, the one named last changes fastest.
Arguments:
- token_ids: int32 [32, 4], replicated, may hold values from 0 to 32767
- lengths: int32 [32], P('replica'), may hold values from 2 to 4096, as said below
- embed: bfloat16 [32768, 6144], P(('replica', 'tensor')), may hold values from -200 to 200
- kv_cache: bfloat16 [8, 32, 4096, 256], P('replica', 'tensor'), may hold values from -170 to 170
- qkv_weight: bfloat16 [6144, 8192], P(None, 'tensor'), may hold values from -0.078125 to 0.078125
- out_weight: bfloat16 [6144, 6144], P('tensor'), may hold values from -0.078125 to 0.078125
- new_qkv: float32 [24576, 2048], P(('replica', 'tensor')), may hold values from -0.078125 to 0.078125
- pushed_qkv: bfloat16 [24576, 2048], P(('replica', 'tensor')), may hold values from -0.078125 to 0.078125
- resid_qkv: float32 [24576, 2048], P(('replica', 'tensor')), may hold values from -0.078125 to 0.078125
- qkv_map: int32 [24576], P(('replica', 'tensor')), may hold values from 0 to 24575, as said below
- new_out: float32 [18432, 2048], P(('replica', 'tensor')), may hold values from -0.078125 to 0.078125
- pushed_out: bfloat16 [18432, 2048], P(('replica', 'tensor')), may hold values from -0.078125 to 0.078125
- resid_out: float32 [18432, 2048], P(('replica', 'tensor')), may hold values from -0.078125 to 0.078125
- out_map: int32 [18432], P(('replica', 'tensor')), may hold values from 0 to 18431, as said below
Outputs:
- attn_out: bfloat16 [32, 4, 6144], P('replica', None, 'tensor')
Inputs may be any that keep to these rules, and one draw needn't show every extreme that they name: `qkv_map`: A permutation of all slot numbers. The 192 slots of one device hold exactly 18 blocks of column block t for half of the tensor indices t and exactly 6 for the others. `out_map`: A permutation of all slot numbers. The 144 slots of one device hold exactly 13 blocks of row block t for half of the tensor indices t and exactly 5 for the others. `lengths`: each aligned run of 4 rows (one replica) holds a row of length 4096.
All inputs are finite; a program needn't handle non-finite values.
Results may differ from a plain program's by a relative error of at most 0.02.
The roundings to bfloat16 on the way count: a program that leaves them out, or rounds other values in their place, can miss the bound.
Values may be sent and summed in bfloat16 or wider, within the bound.
No kernel may reach another device: no remote copies, remote signals or barrier semaphores. Data moves between devices by JAX's collectives and lax.ppermute only.
A program may use at most 192 MiB of HBM per device.

v0:
```python
import jax
import jax.numpy as jnp
from jax import lax
from jax.sharding import PartitionSpec as P

D = 6144
QH = 48
KVH = 8
HD = 128
STEPS = 4
CACHE = 4096


THETA = 1000000.0
EPS = 1e-05


def partner(value, axis, apart):
    mask = 2**apart
    pairs = [(source, source ^ mask) for source in range(lax.axis_size(axis))]
    return lax.ppermute(value, axis, pairs)


def rope_tables(positions, full_width):
    half_width = full_width // 2
    inverse_freq = jnp.power(THETA, -(jnp.arange(half_width, dtype=jnp.float32) * 2.0 / full_width))
    angles = positions.astype(jnp.float32)[..., None] * inverse_freq
    return (jnp.cos(angles), jnp.sin(angles))


def rotate(vector, cos_table, sin_table):
    half_width = vector.shape[-1] // 2
    lower_part = vector[..., :half_width]
    upper_part = vector[..., half_width:]
    return jnp.concatenate(
        [
            lower_part * cos_table - upper_part * sin_table,
            upper_part * cos_table + lower_part * sin_table,
        ],
        axis=-1,
    )


def send_blocks(new_rows, pushed_rows, resid_rows, block_ids, local_count):
    tensors = lax.axis_size("tensor")
    replicas = lax.axis_size("replica")
    owned_rows = new_rows.shape[0]
    block_width = new_rows.shape[1]
    mean_load = owned_rows // tensors
    capacity = mean_load + mean_load // 2
    payload = (new_rows - pushed_rows.astype(jnp.float32) + resid_rows).astype(jnp.bfloat16)
    target = block_ids // local_count
    hit_table = (target[:, None] == jnp.arange(tensors)[None, :]).astype(jnp.int32)
    before = jnp.cumsum(hit_table, axis=0) - hit_table
    position = jnp.sum(before * hit_table, axis=1)
    slot_pos = target * capacity + position
    packed = jnp.zeros((tensors * capacity, block_width), jnp.bfloat16).at[slot_pos].set(payload)
    labels = jnp.full((tensors * capacity,), -1, jnp.int32).at[slot_pos].set(block_ids)
    packed = packed.reshape(tensors, capacity, block_width)
    labels = labels.reshape(tensors, capacity)
    copies = jnp.broadcast_to(packed[None], (replicas, tensors, capacity, block_width)).reshape(
        replicas * tensors, capacity, block_width
    )
    copy_ids = jnp.broadcast_to(labels[None], (replicas, tensors, capacity)).reshape(
        replicas * tensors, capacity
    )
    arrived, arrived_ids = (
        lax.all_to_all(copies, ("replica", "tensor"), split_axis=0, concat_axis=0, tiled=True),
        lax.all_to_all(copy_ids, ("replica", "tensor"), split_axis=0, concat_axis=0, tiled=True),
    )
    first_block = lax.axis_index("tensor") * local_count
    local_index = jnp.where(arrived_ids >= 0, arrived_ids - first_block, local_count).reshape(-1)
    placed = jnp.zeros((local_count, block_width), jnp.bfloat16)
    return placed.at[local_index].set(arrived.reshape(-1, block_width), mode="drop")


def body(
    token_ids,
    lengths,
    embed,
    kv_cache,
    qkv_weight,
    out_weight,
    new_qkv,
    pushed_qkv,
    resid_qkv,
    qkv_map,
    new_out,
    pushed_out,
    resid_out,
    out_map,
):
    tensors = lax.axis_size("tensor")
    splits = tensors // KVH
    per_dev = QH // tensors
    group_size = QH // KVH
    half_dim = HD // splits
    rows_here = lengths.shape[0]
    rows_mine = rows_here // splits
    owner_index = lax.axis_index(("replica", "tensor"))
    vocab_part = embed.shape[0]
    ids_flat = token_ids.reshape(-1)
    shifted = ids_flat - owner_index * vocab_part
    onehot = (shifted[:, None] == jnp.arange(vocab_part)[None, :]).astype(jnp.bfloat16)
    lookup_terms = jnp.dot(onehot, embed, preferred_element_type=jnp.float32)
    summed = lax.psum(lookup_terms, ("replica", "tensor"))
    own_rows = lax.dynamic_slice_in_dim(
        summed, lax.axis_index("replica") * rows_here * STEPS, rows_here * STEPS, 0
    )
    normed = (
        own_rows * lax.rsqrt(jnp.mean(own_rows * own_rows, axis=-1, keepdims=True) + EPS)
    ).astype(jnp.bfloat16)
    qkv_delta = send_blocks(
        new_qkv, pushed_qkv, resid_qkv, qkv_map, qkv_weight.size // new_qkv.shape[1]
    )
    qkv_new = (
        qkv_weight.astype(jnp.float32) + qkv_delta.reshape(qkv_weight.shape).astype(jnp.float32)
    ).astype(jnp.bfloat16)
    projected = jnp.dot(normed, qkv_new, preferred_element_type=jnp.float32).astype(jnp.bfloat16)
    query_own = projected[:, : per_dev * HD]
    keyval_own = projected[:, per_dev * HD :]
    member = lax.axis_index("tensor") % splits
    query_other, keyval_other = partner((query_own, keyval_own), "tensor", 0)
    is_first = member == 0
    query_all = jnp.where(
        is_first,
        jnp.concatenate([query_own, query_other], axis=1),
        jnp.concatenate([query_other, query_own], axis=1),
    )
    key_all = jnp.where(
        is_first,
        jnp.concatenate([keyval_own[:, :half_dim], keyval_other[:, :half_dim]], axis=1),
        jnp.concatenate([keyval_other[:, :half_dim], keyval_own[:, :half_dim]], axis=1),
    )
    value_all = jnp.where(
        is_first,
        jnp.concatenate([keyval_own[:, half_dim:], keyval_other[:, half_dim:]], axis=1),
        jnp.concatenate([keyval_other[:, half_dim:], keyval_own[:, half_dim:]], axis=1),
    )
    row_start = member * rows_mine
    query_rows = lax.dynamic_slice_in_dim(
        query_all, row_start * STEPS, rows_mine * STEPS, 0
    ).reshape(rows_mine, STEPS, group_size, HD)
    key_rows = lax.dynamic_slice_in_dim(key_all, row_start * STEPS, rows_mine * STEPS, 0).reshape(
        rows_mine, STEPS, HD
    )
    value_rows = lax.dynamic_slice_in_dim(
        value_all, row_start * STEPS, rows_mine * STEPS, 0
    ).reshape(rows_mine, STEPS, HD)
    row_lengths = lax.dynamic_slice_in_dim(lengths, row_start, rows_mine, 0)
    positions = row_lengths[:, None] + jnp.arange(STEPS, dtype=jnp.int32)[None, :]
    cos_table, sin_table = rope_tables(positions, HD)
    query_rot = rotate(
        query_rows.astype(jnp.float32), cos_table[:, :, None], sin_table[:, :, None]
    ).astype(jnp.bfloat16)
    key_rot = rotate(key_rows.astype(jnp.float32), cos_table, sin_table).astype(jnp.bfloat16)
    cache_rows = kv_cache[0]
    score_scale = HD ** (-0.5)
    cache_scores = (
        jnp.einsum(
            "rjhd,rpd->rjhp", query_rot, cache_rows[..., :HD], preferred_element_type=jnp.float32
        )
        * score_scale
    )
    valid_mask = jnp.arange(CACHE)[None, :] < row_lengths[:, None]
    cache_scores = jnp.where(valid_mask[:, None, None, :], cache_scores, -1e30)
    fresh_scores = (
        jnp.einsum("rjhd,rkd->rjhk", query_rot, key_rot, preferred_element_type=jnp.float32)
        * score_scale
    )
    causal = jnp.arange(STEPS)[None, :] <= jnp.arange(STEPS)[:, None]
    fresh_scores = jnp.where(causal[None, :, None, :], fresh_scores, -1e30)
    row_top = jnp.maximum(jnp.max(cache_scores, axis=-1), jnp.max(fresh_scores, axis=-1))[..., None]
    cache_exp = jnp.exp(cache_scores - row_top)
    fresh_exp = jnp.exp(fresh_scores - row_top)
    row_total = jnp.sum(cache_exp, axis=-1) + jnp.sum(fresh_exp, axis=-1)
    mixture = jnp.einsum(
        "rjhp,rpd->rjhd",
        cache_exp.astype(jnp.bfloat16),
        cache_rows[..., HD:],
        preferred_element_type=jnp.float32,
    )
    mixture = mixture + jnp.einsum(
        "rjhk,rkd->rjhd",
        fresh_exp.astype(jnp.bfloat16),
        value_rows,
        preferred_element_type=jnp.float32,
    )
    attended = (mixture / row_total[..., None]).astype(jnp.bfloat16)
    kept = lax.dynamic_slice_in_dim(attended, member * per_dev, per_dev, 2)
    given = lax.dynamic_slice_in_dim(attended, (1 - member) * per_dev, per_dev, 2)
    received = partner(given, "tensor", 0)
    head_rows = jnp.where(
        member == 0,
        jnp.concatenate([kept, received], axis=0),
        jnp.concatenate([received, kept], axis=0),
    )
    head_rows = head_rows.reshape(rows_here * STEPS, per_dev * HD)
    out_delta = send_blocks(
        new_out, pushed_out, resid_out, out_map, out_weight.size // new_out.shape[1]
    )
    out_new = (
        out_weight.astype(jnp.float32) + out_delta.reshape(out_weight.shape).astype(jnp.float32)
    ).astype(jnp.bfloat16)
    partial_out = jnp.dot(head_rows, out_new, preferred_element_type=jnp.float32).reshape(
        rows_here, STEPS, D
    )
    summed_out = lax.psum_scatter(
        partial_out.astype(jnp.bfloat16), "tensor", scatter_dimension=2, tiled=True
    )
    return summed_out


def solution(mesh):
    return jax.shard_map(
        body,
        mesh=mesh,
        in_specs=(
            P(),
            P("replica"),
            P(("replica", "tensor"), None),
            P("replica", "tensor", None, None),
            P(None, "tensor"),
            P("tensor", None),
            P(("replica", "tensor"), None),
            P(("replica", "tensor"), None),
            P(("replica", "tensor"), None),
            P(("replica", "tensor")),
            P(("replica", "tensor"), None),
            P(("replica", "tensor"), None),
            P(("replica", "tensor"), None),
            P(("replica", "tensor")),
        ),
        out_specs=P("replica", None, "tensor"),
        check_vma=False,
    )
```

profile of v0, /device:TPU:0, one launch (start us, length us, event | category | flops | bytes accessed | tf_op | source)
XLA Modules:
  0.0 673.0 jit_solution(11461894918559843184)
XLA Ops:
  6.5 0.8 and_select_fusion
  7.4 0.6 reduce-window.16
  8.0 0.2 slice_reduce_fusion
  8.3 0.7 compare_select_fusion.4
  9.0 1.2 scatter_custom_fusion.3
  10.2 0.1 broadcast_in_dim.130
  10.3 0.6 broadcast_in_dim.131
  10.9 11.1 %all-to-all-start.2 = ((s32[128,1,13]{2,1,0:T(1,128)}), s32[128,1,13]{2,1,0:T(1,128)S(1)}, u32[]{:S(2)}, u32[]{:S(2)}) async-start(s32[128,1,13]{2,1,0:T(1,128)} %bitcast.16), calls=%async_computation.2 | async-start | bytes 131072 | tf_op jit(solution)/shard_map/all_to_all | solution.py:69
  22.1 0.7 and_select_fusion.1
  22.8 0.6 reduce-window.14
  23.4 0.2 slice_reduce_fusion.1
  23.7 0.7 compare_select_fusion.5
  24.4 1.4 scatter_custom_fusion
  25.8 0.1 broadcast_in_dim.117
  25.9 5.4 all-to-all-done.2
  31.3 0.6 broadcast_in_dim.118
  31.9 4.8 all-to-all-start
  36.7 4.5 scatter_custom_fusion.1
  41.2 2.4 broadcast_in_dim.122
  43.6 2.3 all-to-all-done
  45.9 7.5 %broadcast_in_dim.123 = bf16[8,16,18,2048]{3,2,1,0:T(8,128)(2,1)} broadcast(bf16[16,18,2048]{2,1,0:T(8,128)(2,1)} %broadcast_in_dim.122), dimensions={1,2,3} | broadcast | bytes 10616832 | tf_op jit(solution)/shard_map/broadcast_in_dim | solution.py:61
  53.4 8.0 %all-to-all-start.1 = ((bf16[128,18,2048]{2,1,0:T(8,128)(2,1)}), bf16[128,18,2048]{2,1,0:T(8,128)(2,1)}, u32[]{:S(2)}, u32[]{:S(2)}) async-start(bf16[128,18,2048]{2,1,0:T(8,128)(2,1)} %bitcast.63), calls=%async_computation.1 | async-start | bytes 25165824 | tf_op jit(solution)/shard_map/all_to_all | solution.py:68
  61.4 3.7 scatter_custom_fusion.4
  65.1 2.5 broadcast_in_dim.135
  67.6 152.3 %all-to-all-done.1 = bf16[128,18,2048]{2,1,0:T(8,128)(2,1)} async-done(((bf16[128,18,2048]{2,1,0:T(8,128)(2,1)}), bf16[128,18,2048]{2,1,0:T(8,128)(2,1)}, u32[]{:S(2)}, u32[]{:S(2)}) %all-to-all-start.1) | async-done | bytes 9437216 | tf_op jit(solution)/shard_map/all_to_all | solution.py:68
  219.9 5.7 broadcast_in_dim.136
  225.6 16.4 %all-to-all-start.3 = ((bf16[128,13,2048]{2,1,0:T(8,128)(2,1)}), bf16[128,13,2048]{2,1,0:T(8,128)(2,1)}, u32[]{:S(2)}, u32[]{:S(2)}) async-start(bf16[128,13,2048]{2,1,0:T(8,128)(2,1)} %bitcast.64), calls=%async_computation.3 | async-start | bytes 16777216 | tf_op jit(solution)/shard_map/all_to_all | solution.py:68
  242.0 0.1 copy.21
  242.1 0.1 sub.94
  242.3 2.3 fusion.22
  244.5 0.2 reduce-scatter.4.cloned.1.call-start
  244.8 0.1 dynamic_slice.21
  245.0 0.1 iota_compare_fusion.2
  245.1 0.2 fusion.24
  245.3 0.2 select_n.157
  245.5 0.2 fusion.23
  245.7 0.1 select_n.141
  245.9 234.4 %all-reduce.4.cloned.1.call-done = f32[128,6144]{1,0:T(8,128)} async-done(((f32[128,6144]{1,0:T(8,128)}), f32[128,6144]{1,0:T(8,128)}) %all-reduce.4.cloned.1.call-update) | async-done | bytes 3145744 | tf_op jit(solution)/shard_map/psum | solution.py:106
  480.4 1.2 multiply_reduce_fusion
  481.5 14.1 %reshape.269 = bf16[2304,2048]{1,0:T(8,128)(2,1)} reshape(bf16[128,18,2048]{2,1,0:T(8,128)(2,1)} %all-to-all-done.1) | data formatting | bytes 18874368 | tf_op jit(solution)/shard_map/reshape | solution.py:74
  495.6 20.5 %scatter_custom_fusion.2 = bf16[1536,2048]{1,0:T(8,128)(2,1)} fusion(s32[2304]{0:T(1024)S(1)} %fusion.36, bf16[2304,2048]{1,0:T(8,128)(2,1)} %reshape.269, bf16[]{:T(256)} %constant.43.clone.1), kind=kCustom, calls=%fused_computation.13 | custom fusion | bytes 6291968 | tf_op jit(solution)/shard_map/scatter | solution.py:74
  516.0 11.6 %reshape.244 = f32[6144,512]{1,0:T(8,128)} reshape(bf16[1536,2048]{1,0:T(8,128)(2,1)} %scatter_custom_fusion.2) | data formatting | bytes 18874368 | tf_op jit(solution)/shard_map/convert_element_type | solution.py:117
  527.6 7.6 %fusion.11 = bf16[16,512]{1,0:T(8,128)(2,1)S(1)} fusion(f32[6144,512]{1,0:T(8,128)} %reshape.244, bf16[6144,512]{1,0:T(8,128)(2,1)} %param.18, f32[128,6144]{1,0:T(8,128)} %all-reduce.4.cloned.1.call-done, s32[]{:T(128)S(6)} %select_n.137, f32[16]{0:T(128)S(1)} %add_rsqrt_fusion), kind=kOutput, calls=%fused_computation.25 | convolution fusion | flops 110305280 | bytes 19284036 | tf_op jit(solution)/shard_map/dot_general | solution.py:119
  535.3 0.1 fusion.55
  535.3 0.5 collective-permute-start
  535.9 0.6 collective-permute-done.1
  536.5 0.1 fusion.42
  536.6 0.1 subtract_convert_fusion.1
  536.8 0.1 subtract_convert_fusion
  536.9 0.3 fusion.58
  537.1 2.6 fusion.57
  539.8 0.3 fusion.13
  540.1 0.6 fusion.8
  540.8 0.2 fusion.10
  541.0 0.6 collective-permute-start.2
  541.6 9.3 %reshape.293 = bf16[1664,2048]{1,0:T(8,128)(2,1)} reshape(bf16[128,13,2048]{2,1,0:T(8,128)(2,1)} %all-to-all-done.3) | data formatting | bytes 13631488 | tf_op jit(solution)/shard_map/reshape | solution.py:74
  550.9 16.8 %scatter_custom_fusion.5 = bf16[1152,2048]{1,0:T(8,128)(2,1)} fusion(s32[1664]{0:T(1024)S(1)} %fusion.39, bf16[1664,2048]{1,0:T(8,128)(2,1)} %reshape.293, bf16[]{:T(256)} %constant.43.clone.1), kind=kCustom, calls=%fused_computation.15 | custom fusion | bytes 4719104 | tf_op jit(solution)/shard_map/scatter | solution.py:74
  567.6 8.3 %reshape.248 = f32[384,6144]{1,0:T(8,128)} reshape(bf16[1152,2048]{1,0:T(8,128)(2,1)} %scatter_custom_fusion.5) | data formatting | bytes 14155776 | tf_op jit(solution)/shard_map/convert_element_type | solution.py:203
  576.0 6.0 convolution_convert_fusion
  582.0 6.4 copy.30
  588.5 8.4 %reshape.306 = bf16[6144,16]{1,0:T(8,128)(2,1)} reshape(bf16[6144,4,4]{2,1,0:T(4,128)(2,1)} %bitcast.65) | data formatting | bytes 393216
  596.9 67.3 %reduce-scatter.4.cloned.1.call-done = bf16[384,16]{1,0:T(8,128)(2,1)} async-done(((bf16[6144,16]{1,0:T(8,128)(2,1)}), bf16[384,16]{1,0:T(8,128)(2,1)}) %reduce-scatter.4.cloned.1.call-update) | async-done | bytes 12304
  664.2 1.1 reshape.307
  665.3 0.9 copy.31
  (48 shorter events, 0.8 us)
Async XLA Ops:
  6.5 235.7 %copy-start = (bf16[256,6144]{1,0:T(8,128)(2,1)S(1)}, bf16[256,6144]{1,0:T(8,128)(2,1)}, u32[]{:S(2)}) copy-start(bf16[256,6144]{1,0:T(8,128)(2,1)} %param.16) | copy-start | bytes 9437188
  10.9 20.3 %all-to-all-start.2 = ((s32[128,1,13]{2,1,0:T(1,128)}), s32[128,1,13]{2,1,0:T(1,128)S(1)}, u32[]{:S(2)}, u32[]{:S(2)}) async-start(s32[128,1,13]{2,1,0:T(1,128)} %bitcast.16), calls=%async_computation.2 | async-start | bytes 131072 | tf_op jit(solution)/shard_map/all_to_all | solution.py:69
  31.9 14.0 %all-to-all-start = ((s32[128,1,18]{2,1,0:T(1,128)}), s32[128,1,18]{2,1,0:T(1,128)S(1)}, u32[]{:S(2)}, u32[]{:S(2)}) async-start(s32[128,1,18]{2,1,0:T(1,128)} %bitcast.1), calls=%async_computation | async-start | bytes 131072 | tf_op jit(solution)/shard_map/all_to_all | solution.py:69
  53.4 166.5 %all-to-all-start.1 = ((bf16[128,18,2048]{2,1,0:T(8,128)(2,1)}), bf16[128,18,2048]{2,1,0:T(8,128)(2,1)}, u32[]{:S(2)}, u32[]{:S(2)}) async-start(bf16[128,18,2048]{2,1,0:T(8,128)(2,1)} %bitcast.63), calls=%async_computation.1 | async-start | bytes 25165824 | tf_op jit(solution)/shard_map/all_to_all | solution.py:68
  225.6 16.4 %copy-start.3 = (s32[32,4]{0,1:T(4,128)S(1)}, s32[32,4]{0,1:T(4,128)}, u32[]{:S(2)}) copy-start(s32[32,4]{0,1:T(4,128)} %param.14) | copy-start | bytes 1540
  225.6 316.0 %all-to-all-start.3 = ((bf16[128,13,2048]{2,1,0:T(8,128)(2,1)}), bf16[128,13,2048]{2,1,0:T(8,128)(2,1)}, u32[]{:S(2)}, u32[]{:S(2)}) async-start(bf16[128,13,2048]{2,1,0:T(8,128)(2,1)} %bitcast.64), calls=%async_computation.3 | async-start | bytes 16777216 | tf_op jit(solution)/shard_map/all_to_all | solution.py:68
  242.0 238.4 %all-reduce.4.cloned.1.call-start = ((), (), s32[]{:S(2)}) async-start(), calls=%async_computation.5 | async-start | bytes 6291456 | tf_op jit(solution)/shard_map/psum | solution.py:106
  242.2 2.6 copy-start.4
  244.5 419.7 %reduce-scatter.4.cloned.1.call-start = ((), (), s32[]{:S(2)}) async-start(), calls=%async_computation.6 | async-start | bytes 1671168
  535.3 1.2 collective-permute-start.1
  535.3 1.4 collective-permute-start
  536.8 3.4 copy-start.2
  541.0 35.0 %collective-permute-start.2 = (bf16[2,4,3,128]{3,2,1,0:T(4,128)(2,1)S(1)}, bf16[2,4,3,128]{3,2,1,0:T(4,128)(2,1)S(1)}, u32[]{:S(2)}, u32[]{:S(2)}) collective-permute-start(bf16[2,4,3,128]{3,2,1,0:T(4,128)(2,1)S(1)} %get-tuple-element.8), channel_id=1, source_target_pairs={{0,1},{1,0},{2,3},{3,2},{4,5},{5,4},{6,7},{7,6},{8,9},{9,8},{10,11... | collective-permute-start | bytes 18440 | tf_op jit(solution)/shard_map/ppermute | solution.py:21
  588.5 77.7 %copy-start.1 = (bf16[256,6144]{1,0:T(8,128)(2,1)S(1)}, bf16[256,6144]{1,0:T(8,128)(2,1)}, u32[]{:S(2)}) copy-start(bf16[256,6144]{1,0:T(8,128)(2,1)} %param.16) | copy-start | bytes 9437188
Sparse Core Ops, SparseCore 0:
  247.5 232.7 all-reduce.3
  597.0 67.1 reduce-scatter.3
where the time goes:
time: 675 us; the launch traced here: 673 us
  waiting for transfers between devices  462 us (68%)
  local copies, waits for them, and re-layouts  120 us (18%)
  starting transfers between devices  41.7 us (6%)
  matrix products  19.6 us (3%)
  other arithmetic  15.2 us (2%)
  between operations  13.7 us (2%)
    psum x1, waiting for transfers between devices, body(): summed = lax.psum(lookup_terms, ('replica', 'tensor'))  234 us
    all_to_all x2, waiting for transfers between devices, send_blocks(): lax.all_to_all(copies, ('replica', 'tensor'), split_axis=0, concat_axis=0...  152 us
    unnamed x3, waiting for transfers between devices  67.4 us
    scatter x2, local copies, waits for them, and re-layouts, send_blocks(): placed.at[local_index].set(arrived.reshape(-1, block_width), mode='drop')  37.2 us
    all_to_all x2, starting transfers between devices, send_blocks(): lax.all_to_all(copies, ('replica', 'tensor'), split_axis=0, concat_axis=0...  24.3 us
    reshape x2, local copies, waits for them, and re-layouts, send_blocks(): arrived.reshape(-1, block_width)  23.3 us
    broadcast_in_dim x4, local copies, waits for them, and re-layouts, send_blocks(): jnp.broadcast_to(packed[None], (replicas, tensors, capacity, block_width))  18.1 us
    unnamed x14, local copies, waits for them, and re-layouts  16.8 us
  transfers between devices with their start and end apart: 9, of which 6 were waited for; matrix products, arithmetic and copies ran while one was open for 17% of the time, Pallas kernels for 0%

commit v1 on v0

v1 whole, which is shorter than its diff:
```python
import functools

import jax
import jax.numpy as jnp
from jax import lax
from jax.experimental import pallas as pl
from jax.experimental.pallas import tpu as pltpu
from jax.sharding import PartitionSpec as P

D = 6144
QH = 48
KVH = 8
HD = 128
STEPS = 4
CACHE = 4096
THETA = 1000000.0
EPS = 1e-05

AXES = ("replica", "tensor")
NT = 16
BLOCK = 2048
WIDE = BLOCK + 128
QKV_CAP = 18
SLOTS = 32
KC = D // 8
OC = D // 16

CORE, XHI, Z, Y, XLO = 0, 1, 2, 4, 6


def swap(value, mask):
    return lax.ppermute(value, AXES, [(i, i ^ mask) for i in range(128)])


def f32dot(a, b):
    return jnp.dot(a, b, preferred_element_type=jnp.float32)


def dot_t(a, b):
    return lax.dot_general(a, b, (((1,), (1,)), ((), ())), preferred_element_type=jnp.float32)


def iota(shape, dim):
    return lax.broadcasted_iota(jnp.int32, shape, dim)


def call(kernel, name, out_shape, operands, specs=None, scratch=(), mib=16, flops=0, moved=0):
    specs = specs or {}
    vmem = pl.BlockSpec(memory_space=pltpu.VMEM)
    return pl.pallas_call(
        kernel,
        out_shape=out_shape,
        in_specs=[specs.get(i, vmem) for i in range(len(operands))],
        scratch_shapes=list(scratch),
        compiler_params=pltpu.CompilerParams(vmem_limit_bytes=mib * 1024 * 1024),
        cost_estimate=pl.CostEstimate(flops=flops, bytes_accessed=moved, transcendentals=0),
        name=name,
    )(*operands)


SMEM = pl.BlockSpec(memory_space=pltpu.SMEM)
ANY = pl.BlockSpec(memory_space=pl.ANY)


def shape16(*dims):
    return jax.ShapeDtypeStruct(dims, jnp.bfloat16)


def unshuffle(dtype):
    d = iota((256, 256), 1)
    return (iota((256, 256), 0) == (d & 63) * 4 + (d >> 6)).astype(dtype)


def embed_kernel(other, pos, ids_ref, embed_ref, after, out_ref, buf, sem):
    half = pos[4] ^ other
    copies = []
    for s in range(4):
        start = pl.multiple_of((half * 4 + (pos[2] ^ s)) * KC, KC)
        copies.append(
            pltpu.make_async_copy(embed_ref.at[:, pl.ds(start, KC)], buf.at[s], sem.at[s])
        )
        copies[-1].start()
    place = iota((128, 32), 0)
    row = ((place >> 5) ^ pos[3]) * 8 + ((place & 31) >> 2)
    pick = (iota((128, 32), 1) == row).astype(jnp.bfloat16)
    ids = ids_ref[...]
    high, low = ids >> 8, ids & 255
    wide = f32dot(pick, high.astype(jnp.float32).astype(jnp.bfloat16)) * 256.0 + f32dot(
        pick, low.astype(jnp.float32).astype(jnp.bfloat16)
    )
    step = iota((128, 4), 0) & 3
    mine = jnp.sum(jnp.where(iota((128, 4), 1) == step, wide, 0.0), axis=1, keepdims=True)
    local = mine.astype(jnp.int32) - pos[5]
    onehot = (iota((128, embed_ref.shape[0]), 1) == local).astype(jnp.bfloat16)
    for s in range(4):
        copies[s].wait()
        out_ref[s] = f32dot(onehot, buf[s]).astype(jnp.bfloat16)


def embed_half(pos, ids, embed, after, other):
    vocab = embed.shape[0]
    return call(
        functools.partial(embed_kernel, other),
        "embed_part",
        shape16(4, 128, KC),
        (pos, ids, embed, after),
        {0: SMEM, 2: ANY, 3: ANY},
        [pltpu.VMEM((4, vocab, KC), jnp.bfloat16), pltpu.SemaphoreType.DMA((4,))],
        mib=56 if other else 16,
        flops=2 * 128 * vocab * KC * 4,
        moved=2 * vocab * KC * 4,
    )


def settle_kernel(a, b, c, d, after, out_ref):
    total = (a[...].astype(jnp.float32) + b[...].astype(jnp.float32)) + (
        c[...].astype(jnp.float32) + d[...].astype(jnp.float32)
    )
    total = total.astype(jnp.bfloat16)
    order = unshuffle(jnp.bfloat16)
    for g in range(KC // 256):
        cols = slice(g * 256, (g + 1) * 256)
        out_ref[:, cols] = f32dot(total[:, cols], order).astype(jnp.bfloat16)


def settle(parts, after):
    return call(
        settle_kernel, "settle", shape16(*parts[0].shape), (*parts, after), {4: ANY}, moved=10**5
    )


def stack_kernel(count, *refs):
    out_ref = refs[-1]
    rows = refs[0].shape[0]
    for k in range(count):
        out_ref[k * rows : (k + 1) * rows, :] = refs[k][...]


def stack_after(parts, *after):
    rows, columns = parts[0].shape
    n = len(parts)
    return call(
        functools.partial(stack_kernel, n),
        "stack",
        shape16(n * rows, columns),
        (*parts, *after),
        {n + i: ANY for i in range(len(after))},
        moved=10**5,
    )


def split_qkv(ids):
    q = ids >> 9
    t = (q * 171) >> 9
    return t, ids - t * 1536


def split_out(ids):
    q = ids >> 7
    t = (q * 57) >> 9
    local = ids - t * 1152
    row = (local * 21846) >> 16
    return t, 1536 + (local - row * 3) * 384 + row


def slots_of(ids, split, first):
    n = ids.shape[1]
    target, place = split(ids)
    hit = iota((NT, n), 0) == target
    earlier = (iota((n, n), 0) < iota((n, n), 1)).astype(jnp.bfloat16)
    before = f32dot(hit.astype(jnp.bfloat16), earlier)
    rank = jnp.sum(jnp.where(hit, before, 0.0), axis=0, keepdims=True)
    slot = target * SLOTS + first + rank.astype(jnp.int32)
    chosen = (iota((NT * SLOTS, n), 0) == slot).astype(jnp.bfloat16)
    code = place + 1
    high = code >> 6
    part = iota((128, n), 0)
    label = jnp.where(part == 0, high, jnp.where(part == 1, code - high * 64, 0))
    return chosen, label.astype(jnp.float32).astype(jnp.bfloat16)


def pack_kernel(ids_a, ids_b, *refs):
    sources, out_ref, bufs, sem = refs[:6], refs[6], refs[7:13], refs[13]
    copies = []
    for q in range(4):
        cols = slice(q * 512, (q + 1) * 512)
        for k in range(6):
            copies.append(
                pltpu.make_async_copy(
                    sources[k].at[:, cols], bufs[k].at[:, cols], sem.at[q * 6 + k]
                )
            )
            copies[-1].start()
    chosen_a, label_a = slots_of(ids_a[...], split_qkv, 0)
    chosen_b, label_b = slots_of(ids_b[...], split_out, QKV_CAP)
    out_ref[:, BLOCK:] = (dot_t(chosen_a, label_a) + dot_t(chosen_b, label_b)).astype(jnp.bfloat16)

    def payload(new, pushed, resid, cols):
        value = new[:, cols] - pushed[:, cols].astype(jnp.float32) + resid[:, cols]
        return value.astype(jnp.bfloat16)

    for q in range(4):
        cols = slice(q * 512, (q + 1) * 512)
        for k in range(6):
            copies[q * 6 + k].wait()
        packed = f32dot(chosen_a, payload(*bufs[:3], cols))
        packed = packed + f32dot(chosen_b, payload(*bufs[3:], cols))
        out_ref[:, cols] = packed.astype(jnp.bfloat16)


def pack(ids_a, ids_b, *sources):
    owned = sources[0].shape[0] + sources[3].shape[0]
    return call(
        pack_kernel,
        "pack_blocks",
        shape16(NT * SLOTS, WIDE),
        (ids_a.reshape(1, -1), ids_b.reshape(1, -1), *sources),
        {k: ANY for k in range(2, 8)},
        [pltpu.VMEM(source.shape, source.dtype) for source in sources]
        + [pltpu.SemaphoreType.DMA((24,))],
        mib=56,
        flops=2 * NT * SLOTS * owned * BLOCK,
        moved=owned * BLOCK * 10,
    )


def places(labels):
    lane = iota((8, 128), 1)
    scale = jnp.where(lane == 0, 64.0, jnp.where(lane == 1, 1.0, 0.0)).astype(jnp.bfloat16)
    return dot_t(scale, labels)[0:1, :].astype(jnp.int32) - 1


def place_qkv_kernel(other, pos, arrived_ref, weight_ref, out_ref):
    half = pos[4] ^ other
    here = pos[1] == half
    count = arrived_ref.shape[0]
    where = places(arrived_ref[:, BLOCK:])
    onehot = (iota((768, count), 0) + half * 768 == where).astype(jnp.bfloat16)
    for j in range(4):
        block = f32dot(onehot, arrived_ref[:, j * 512 : (j + 1) * 512]).astype(jnp.bfloat16)
        for g in range(12):
            out_ref[g * 256 + j * 64 : g * 256 + (j + 1) * 64, :] = block[g * 64 : (g + 1) * 64, :]

    @pl.when(here)
    def _():
        order = unshuffle(jnp.float32).T.astype(jnp.bfloat16)
        for g in range(3):
            weight = f32dot(order, weight_ref[g * 256 : (g + 1) * 256, :])
            rows = pl.ds(pl.multiple_of(pos[2] * 768 + g * 256, 256), 256)
            out_ref[rows, :] = (out_ref[rows, :].astype(jnp.float32) + weight).astype(jnp.bfloat16)


def place_qkv(pos, arrived, weight, other):
    return call(
        functools.partial(place_qkv_kernel, other),
        "place_qkv",
        shape16(D // 2, 512),
        (pos, arrived, weight),
        {0: SMEM},
        flops=2 * 768 * arrived.shape[0] * BLOCK,
        moved=6 * 1024 * 1024,
    )


def place_out_kernel(pos, arrived_ref, weight_ref, out_ref):
    count = arrived_ref.shape[0]
    where = places(arrived_ref[:, BLOCK:])
    for c in range(3):
        onehot = (iota((384, count), 0) + 1536 + c * 384 == where).astype(jnp.bfloat16)
        for q in range(4):
            block = f32dot(onehot, arrived_ref[:, q * 512 : (q + 1) * 512])
            cols = slice(c * BLOCK + q * 512, c * BLOCK + (q + 1) * 512)
            out_ref[:, cols] = block.astype(jnp.bfloat16)
    rows = pl.ds(pl.multiple_of(pos[0] * 48, 48), 48)
    out_ref[rows, :] = (
        out_ref[rows, :].astype(jnp.float32) + weight_ref[...].astype(jnp.float32)
    ).astype(jnp.bfloat16)


def place_out(pos, arrived, weight):
    return call(
        place_out_kernel,
        "place_out",
        shape16(384, D),
        (pos, arrived, weight),
        {0: SMEM},
        flops=2 * 1152 * arrived.shape[0] * BLOCK,
        moved=7 * 1024 * 1024,
    )


def multiply(pos, pieces, matrix_ref, buf, sem):
    copies = []
    for s in range(4):
        start = pl.multiple_of((pos[2] ^ s) * KC, KC)
        copies.append(
            pltpu.make_async_copy(matrix_ref.at[pl.ds(start, KC), :], buf.at[s], sem.at[s])
        )
        copies[-1].start()
    total, squares = 0.0, 0.0
    for s in range(4):
        piece = pieces[s][...]
        wide = piece.astype(jnp.float32)
        squares = squares + jnp.sum(wide * wide, axis=1, keepdims=True)
        copies[s].wait()
        total = total + f32dot(piece, buf[s])
    return total, squares


def project_first_kernel(pos, p0, p1, p2, p3, matrix_ref, total_ref, squares_ref, buf, sem):
    total, squares = multiply(pos, (p0, p1, p2, p3), matrix_ref, buf, sem)
    total_ref[...] = total
    squares_ref[...] = jnp.broadcast_to(squares, squares_ref.shape)


def project_last_kernel(
    pos, p0, p1, p2, p3, matrix_ref, total_ref, squares_ref, o0, o1, o2, o3, buf, sem, work
):
    total, squares = multiply(pos, (p0, p1, p2, p3), matrix_ref, buf, sem)
    total = total + total_ref[...]
    squares = squares + squares_ref[:, 0:1]
    work[...] = total * lax.rsqrt(squares * (1.0 / D) + EPS)
    for s, out_ref in enumerate((o0, o1, o2, o3)):
        rows = []
        for b in range(2):
            for m in range(2):
                x_lo, y, member = pos[1] ^ b, pos[2] ^ s, pos[4] ^ m
                eight = (x_lo * 4 + y) * 2 + member
                start = ((eight >> 2) ^ pos[3]) * 32 + (eight & 3) * 8
                rows.append(work[pl.ds(pl.multiple_of(start, 8), 8), :])
        out_ref[...] = jnp.concatenate(rows, axis=0).astype(jnp.bfloat16)


def project(pos, first, first_matrix, last, last_matrix):
    scratch = [pltpu.VMEM((4, KC, 512), jnp.bfloat16), pltpu.SemaphoreType.DMA((4,))]
    cost = dict(flops=128 * D * 512, moved=4 * 1024 * 1024)
    total, squares = call(
        project_first_kernel,
        "project_first",
        [
            jax.ShapeDtypeStruct((128, 512), jnp.float32),
            jax.ShapeDtypeStruct((128, 128), jnp.float32),
        ],
        (pos, *first, first_matrix),
        {0: SMEM, 5: ANY},
        scratch,
        **cost,
    )
    return call(
        project_last_kernel,
        "project_last",
        [shape16(32, 512)] * 4,
        (pos, *last, last_matrix, total, squares),
        {0: SMEM, 5: ANY},
        scratch + [pltpu.VMEM((128, 512), jnp.float32)],
        **cost,
    )


def share_kernel(other, pos, a0, a1, a2, a3, matrix_ref, out_ref, buf, sem):
    copies = []
    for k in range(8):
        z, x_hi = pos[3] ^ (k // 2), pos[6] ^ (k % 2)
        start = pl.multiple_of((z * 4 + x_hi * 2 + (pos[4] ^ other)) * OC, OC)
        copies.append(
            pltpu.make_async_copy(matrix_ref.at[:, pl.ds(start, OC)], buf.at[k], sem.at[k])
        )
        copies[-1].start()
    heads = jnp.concatenate([a0[...], a1[...], a2[...], a3[...]], axis=0)
    for k in range(8):
        copies[k].wait()
        product = f32dot(heads, buf[k]).astype(jnp.bfloat16)
        for s in range(4):
            out_ref[k // 2, s, k % 2] = product[s * 32 : (s + 1) * 32]


def share_half(pos, heads, matrix, other):
    return call(
        functools.partial(share_kernel, other),
        "share",
        shape16(4, 4, 2, 32, OC),
        (pos, *heads, matrix),
        {0: SMEM, 5: ANY},
        [pltpu.VMEM((8, 384, OC), jnp.bfloat16), pltpu.SemaphoreType.DMA((8,))],
        flops=128 * 384 * D,
        moved=4 * 1024 * 1024,
    )


def add32(parts):
    total = parts[0].astype(jnp.float32)
    for part in parts[1:]:
        total = total + part.astype(jnp.float32)
    return total


def fold_kernel(a, b, c, d, o0, o1, o2, o3):
    total = a[...].astype(jnp.float32) + b[...].astype(jnp.float32)
    total = total + c[...].astype(jnp.float32) + d[...].astype(jnp.float32)
    for k, out_ref in enumerate((o0, o1, o2, o3)):
        out_ref[...] = total[k * 8 : (k + 1) * 8, :].astype(out_ref.dtype)


def fold(parts):
    rows, columns = parts[0].shape
    return call(
        fold_kernel, "fold", [shape16(rows // 4, columns)] * 4, tuple(parts), moved=10**5
    )


def rope_tables(lengths, member):
    half = HD // 2
    inverse_freq = jnp.power(THETA, -(jnp.arange(half, dtype=jnp.float32) * 2.0 / HD))
    row_lengths = lax.dynamic_slice_in_dim(lengths, member * 2, 2, 0)
    positions = (row_lengths[:, None] + jnp.arange(STEPS, dtype=jnp.int32)[None, :]).reshape(-1)
    angles = positions.astype(jnp.float32)[:, None] * inverse_freq
    cos, sin = jnp.cos(angles), jnp.sin(angles)
    return jnp.concatenate([cos, cos], axis=1), jnp.concatenate([-sin, sin], axis=1)


def attend_kernel(pos, lengths, own0, own1, other0, other1, cos_ref, sin_ref, cache, o0, o1):
    member = pos[4]
    own = own0[...].astype(jnp.float32) + own1[...].astype(jnp.float32)
    other = other0[...].astype(jnp.float32) + other1[...].astype(jnp.float32)
    own = own.astype(jnp.bfloat16).astype(jnp.float32)
    other = other.astype(jnp.bfloat16).astype(jnp.float32)
    cos, sin = cos_ref[...], sin_ref[...]

    def rotate(u):
        return (u * cos + pltpu.roll(u, HD // 2, 1) * sin).astype(jnp.bfloat16)

    group = QH // KVH
    heads = [own[:, h * HD : (h + 1) * HD] for h in range(group // 2)]
    heads += [other[:, h * HD : (h + 1) * HD] for h in range(group // 2)]
    query = jnp.concatenate([rotate(u).astype(jnp.float32) for u in heads], axis=0)
    query = query.astype(jnp.bfloat16)
    rest = slice(group // 2 * HD, (group // 2 + 1) * HD)
    first = jnp.where(member == 0, own[:, rest], other[:, rest])
    second = jnp.where(member == 0, other[:, rest], own[:, rest])
    lower = iota((8, HD), 1) < HD // 2
    key = rotate(jnp.where(lower, first, pltpu.roll(second, HD // 2, 1)))
    value = jnp.where(lower, pltpu.roll(first, HD // 2, 1), second).astype(jnp.bfloat16)

    count = group * 8
    scale = HD ** (-0.5)
    token = iota((count, 1), 0) & 7
    upper_row = token >= 4
    length = jnp.where(upper_row, lengths[member * 2 + 1], lengths[member * 2])
    scores = jnp.where(
        upper_row, dot_t(query, cache[0, 1, :, :HD]), dot_t(query, cache[0, 0, :, :HD])
    )
    scores = jnp.where(iota((count, CACHE), 1) < length, scores * scale, -1e30)
    new_token = iota((count, 8), 1)
    seen = ((new_token >> 2) == (token >> 2)) & ((new_token & 3) <= (token & 3))
    fresh = jnp.where(seen, dot_t(query, key) * scale, -1e30)
    top = jnp.maximum(
        jnp.max(scores, axis=1, keepdims=True), jnp.max(fresh, axis=1, keepdims=True)
    )
    scores = jnp.exp(scores - top)
    fresh = jnp.exp(fresh - top)
    total = jnp.sum(scores, axis=1, keepdims=True) + jnp.sum(fresh, axis=1, keepdims=True)
    weights = scores.astype(jnp.bfloat16)
    mixture = jnp.where(
        upper_row, f32dot(weights, cache[0, 1, :, HD:]), f32dot(weights, cache[0, 0, :, HD:])
    )
    mixture = mixture + f32dot(fresh.astype(jnp.bfloat16), value)
    attended = mixture / total
    for k, out_ref in enumerate((o0, o1)):
        blocks = [attended[(k * 3 + h) * 8 : (k * 3 + h + 1) * 8, :] for h in range(3)]
        out_ref[...] = jnp.concatenate(blocks, axis=1).astype(jnp.bfloat16)


def attend(pos, lengths, own, other, tables, kv_cache):
    return call(
        attend_kernel,
        "attend",
        [shape16(8, 384)] * 2,
        (pos, lengths, *own, *other, *tables, kv_cache),
        {0: SMEM, 1: SMEM},
        mib=20,
        flops=8 * 48 * CACHE * HD,
        moved=5 * 1024 * 1024,
    )


def heads_kernel(pos, keep0, got0, keep1, got1, after, out_ref):
    first = pos[4] == 0
    rows = []
    for keep, got in ((keep0, got0), (keep1, got1)):
        a, b = keep[...].astype(jnp.float32), got[...].astype(jnp.float32)
        rows += [jnp.where(first, a, b), jnp.where(first, b, a)]
    out_ref[...] = jnp.concatenate(rows, axis=0).astype(jnp.bfloat16)


def finish_kernel(a, b, c, d, out_ref):
    total = (a[...].astype(jnp.float32) + b[...].astype(jnp.float32)) + (
        c[...].astype(jnp.float32) + d[...].astype(jnp.float32)
    )
    out_ref[...] = total.reshape(out_ref.shape).astype(jnp.bfloat16)


def body(
    token_ids,
    lengths,
    embed,
    kv_cache,
    qkv_weight,
    out_weight,
    new_qkv,
    pushed_qkv,
    resid_qkv,
    qkv_map,
    new_out,
    pushed_out,
    resid_out,
    out_map,
):
    r = lax.axis_index("replica")
    t = lax.axis_index("tensor")
    core = t % 2
    pos = jnp.stack(
        [r, r // 4, r % 4, t // 4, core, (r * NT + t) * embed.shape[0], (t // 2) % 2]
    ).astype(jnp.int32)

    packed = pack(
        qkv_map, out_map, new_qkv, pushed_qkv, resid_qkv, new_out, pushed_out, resid_out
    )
    arrived = lax.all_to_all(packed, "tensor", split_axis=0, concat_axis=0, tiled=True)
    qkv_rows = lax.dynamic_slice_in_dim(qkv_weight, r * 768, 768, 0)
    out_rows = lax.dynamic_slice_in_dim(out_weight, r * 48, 48, 0)
    first_matrix = place_qkv(pos, arrived, qkv_rows, 0)
    last_matrix = place_qkv(pos, arrived, qkv_rows, 1)
    out_part = place_out(pos, arrived, out_rows)

    give = embed_half(pos, token_ids, embed, packed, 1)
    got = swap(give, 1 << CORE)
    keep = embed_half(pos, token_ids, embed, give, 0)
    y_parts = [keep[s] + got[s] for s in range(4)]
    y_got = [swap(y_parts[s], s << Y) for s in range(1, 4)]
    z_all = y_parts[0] + y_got[0] + y_got[1] + y_got[2]
    z_got = [swap(z_all[s * 32 : (s + 1) * 32], s << Z) for s in range(1, 4)]
    x_all = z_all[:32] + z_got[0] + z_got[1] + z_got[2]
    x_masks = [1 << XLO, 1 << XHI, (1 << XLO) | (1 << XHI)]
    mine = settle([x_all] + [swap(x_all, mask) for mask in x_masks], first_matrix)
    z_back = [mine] + [swap(mine, s << Z) for s in range(1, 4)]
    z_rows = stack_after(z_back, last_matrix)
    first = [z_rows] + [swap(z_rows, s << Y) for s in range(1, 4)]
    last = [swap(piece, 1 << CORE) for piece in first]

    shares = project(pos, first, first_matrix, last, last_matrix)
    blocks = fold([shares[0]] + [swap(shares[s], s << Y) for s in range(1, 4)])
    core_bit, x_bit = 1 << CORE, 1 << XLO
    own = (blocks[0], swap(blocks[2], x_bit))
    other = (swap(blocks[1], core_bit), swap(blocks[3], core_bit | x_bit))

    tables = rope_tables(lengths, core)
    head_keep, head_give = attend(pos, lengths, own, other, tables, kv_cache)
    head_pair = call(
        heads_kernel,
        "heads",
        shape16(32, 384),
        (
            pos,
            head_keep,
            swap(head_give, core_bit),
            swap(head_keep, x_bit),
            swap(head_give, core_bit | x_bit),
            out_part,
        ),
        {0: SMEM, 5: ANY},
        moved=10**5,
    )
    heads = [head_pair] + [swap(head_pair, s << Y) for s in range(1, 4)]

    give = share_half(pos, heads, out_part, 1)
    got = swap(give, 1 << CORE)
    keep = share_half(pos, heads, out_part, 0)
    z_parts = [add32([keep[s], got[s]]).astype(jnp.bfloat16) for s in range(4)]
    z_got = [swap(z_parts[s], s << Z) for s in range(1, 4)]
    y_parts = [add32([z_parts[0][s]] + [g[s] for g in z_got]).astype(jnp.bfloat16) for s in range(4)]
    y_got = [swap(y_parts[s], s << Y) for s in range(1, 4)]
    x_parts = add32([y_parts[0]] + y_got).astype(jnp.bfloat16)
    x_got = [
        swap(x_parts[h, b * 16 : (b + 1) * 16], (h << XHI) | (b << XLO))
        for h, b in ((0, 1), (1, 0), (1, 1))
    ]
    return call(
        finish_kernel,
        "finish",
        shape16(lengths.shape[0], STEPS, OC),
        (x_parts[0, :16], *x_got),
        moved=10**5,
    )


def solution(mesh):
    return jax.shard_map(
        body,
        mesh=mesh,
        in_specs=(
            P(),
            P("replica"),
            P(("replica", "tensor"), None),
            P("replica", "tensor", None, None),
            P(None, "tensor"),
            P("tensor", None),
            P(("replica", "tensor"), None),
            P(("replica", "tensor"), None),
            P(("replica", "tensor"), None),
            P(("replica", "tensor")),
            P(("replica", "tensor"), None),
            P(("replica", "tensor"), None),
            P(("replica", "tensor"), None),
            P(("replica", "tensor")),
        ),
        out_specs=P("replica", None, "tensor"),
        check_vma=False,
    )
```

time: 675 us -> 156 us (0.23)
  waiting for transfers between devices: 462 us -> 45.5 us
  local copies, waits for them, and re-layouts: 120 us -> 10.2 us
  Pallas kernels: 0 us -> 35 us
  matrix products: 19.6 us -> 0 us
  starting transfers between devices: 41.7 us -> 61.3 us
  between operations: 13.7 us -> 0.55 us
  other arithmetic: 15.2 us -> 2.63 us
    psum x1 -> x0, waiting for transfers between devices: 234 us -> none  [body(): summed = lax.psum(lookup_terms, ('replica', 'tensor'))]
    all_to_all x4 -> x1, waiting for transfers between devices: 160 us -> 0.01 us  [body(): lax.all_to_all(packed, 'tensor', split_axis=0, concat_axis=0, tiled=True)]
    unnamed x3 -> x0, waiting for transfers between devices: 67.4 us -> none
    ppermute x3 -> x42, starting transfers between devices: 1.11 us -> 53.3 us  [swap(): return lax.ppermute(value, AXES, [(i, i ^ mask) for i in range(128)])]
    ppermute x3 -> x42, waiting for transfers between devices: 0.57 us -> 45.5 us  [swap(): return lax.ppermute(value, AXES, [(i, i ^ mask) for i in range(128)])]
    scatter x4 -> x0, local copies, waits for them, and re-layouts: 39.8 us -> none  [the longest x2 37.2 us: send_blocks(): placed.at[local_index].set(arrived.reshape(-1, block_width), mode='drop')]
    pallas_call x0 -> x16, Pallas kernels: none -> 35 us  [call(): pl.pallas_call(kernel, out_shape=out_shape, in_specs=[specs.get(i, vmem)...]
    all_to_all x4 -> x1, starting transfers between devices: 40.3 us -> 7.97 us  [body(): lax.all_to_all(packed, 'tensor', split_axis=0, concat_axis=0, tiled=True)]
  transfers between devices with their start and end apart: 9 -> 43, of which waited for: 6 -> 20; matrix products, arithmetic and copies ran while one was open for 17% -> 4% of each run, Pallas kernels for 0% -> 13%
where the time goes in v1:
time: 156 us; the launch traced here: 155 us
  starting transfers between devices  61.3 us (39%)
  waiting for transfers between devices  45.5 us (29%)
  Pallas kernels  35 us (22%)
  local copies, waits for them, and re-layouts  10.2 us (7%)
  other arithmetic  2.63 us (2%)
    ppermute x42, starting transfers between devices, swap(): return lax.ppermute(value, AXES, [(i, i ^ mask) for i in range(128)])  53.3 us
    ppermute x42, waiting for transfers between devices, swap(): return lax.ppermute(value, AXES, [(i, i ^ mask) for i in range(128)])  45.5 us
    pallas_call x16, Pallas kernels, call(): pl.pallas_call(kernel, out_shape=out_shape, in_specs=[specs.get(i, vmem)...  35 us
    all_to_all x1, starting transfers between devices, body(): lax.all_to_all(packed, 'tensor', split_axis=0, concat_axis=0, tiled=True)  7.97 us
    unnamed x33, local copies, waits for them, and re-layouts  6.28 us
  transfers between devices with their start and end apart: 43, of which 20 were waited for; matrix products, arithmetic and copies ran while one was open for 4% of the time, Pallas kernels for 13%

profile of v1, /device:TPU:0, one launch (start us, length us, event | category | flops | bytes accessed | tf_op | source)
XLA Modules:
  0.0 155.2 jit_solution(5141564865925210066)
XLA Ops:
  0.0 6.5 %pack_blocks.1.after = bf16[512,2176]{1,0:T(8,128)(2,1)} custom-call(s32[1,192]{1,0:T(1,128)} %bitcast.74, s32[1,144]{1,0:T(1,128)} %bitcast.75, f32[192,2048]{1,0:T(8,128)} %refs_0_.1, bf16[192,2048]{1,0:T(8,128)(2,1)} %refs_1_.1, f32[192,2048]{1,0:T(8,128)} %refs_2_.1, f32[144,2048]{1,0:T(8,128)} %refs_3_.1, bf16[144,2048]{1,0:T(8,128)(2,1)} %refs_4_.1, ...), custom_call_target="tpu_custom_call" | custom-call | flops 704643072 | bytes 6881280 | tf_op jit(solution)/shard_map/pack_blocks/pallas_call | solution.py:50
  6.5 8.0 %all-to-all-start = ((bf16[16,32,2176]{2,1,0:T(8,128)(2,1)}), bf16[16,32,2176]{2,1,0:T(8,128)(2,1)S(1)}, u32[]{:S(2)}, u32[]{:S(2)}) async-start(bf16[16,32,2176]{2,1,0:T(8,128)(2,1)} %bitcast.73), calls=%async_computation | async-start | bytes 4456448 | tf_op jit(solution)/shard_map/all_to_all | solution.py:528
  14.6 0.7 copy.16.ids_ref
  15.2 0.6 stack.32.pos
  15.9 3.8 %embed_part.2.after = bf16[4,128,768]{2,1,0:T(8,128)(2,1)} custom-call(s32[7]{0:T(128)} %stack.32.pos, s32[32,4]{1,0:T(8,128)} %copy.16.ids_ref, bf16[256,6144]{1,0:T(8,128)(2,1)} %embed_ref.3, bf16[512,2176]{1,0:T(8,128)(2,1)} %pack_blocks.1.after), custom_call_target="tpu_custom_call" | custom-call | flops 201326592 | bytes 1572864 | tf_op jit(solution)/shard_map/embed_part/pallas_call | solution.py:50
  20.1 1.1 copy-done.9
  21.2 1.9 %embed_part.3 = bf16[4,128,768]{2,1,0:T(8,128)(2,1)S(1)} custom-call(s32[7]{0:T(128)S(1)} %copy-done.12, s32[32,4]{1,0:T(8,128)S(1)} %copy-done.11, bf16[256,6144]{1,0:T(8,128)(2,1)S(1)} %copy-done.5, bf16[4,128,768]{2,1,0:T(8,128)(2,1)S(1)} %copy-done.9), custom_call_target="tpu_custom_call" | custom-call | flops 201326592 | bytes 1572864 | tf_op jit(solution)/shard_map/embed_part/pallas_call | solution.py:50
  23.2 0.9 copy-done.14
  24.0 0.8 fusion.5
  24.9 1.6 %collective-permute-start.1 = (bf16[128,768]{1,0:T(8,128)(2,1)}, bf16[128,768]{1,0:T(8,128)(2,1)S(1)}, u32[]{:S(2)}, u32[]{:S(2)}) collective-permute-start(bf16[128,768]{1,0:T(8,128)(2,1)} %get-tuple-element.33), channel_id=1, source_target_pairs={{0,16},{1,17},{2,18},{3,19},{4,20},{5,21},{6,22},{7,23},{8,24},{9,... | collective-permute-start | bytes 589832 | tf_op jit(solution)/shard_map/ppermute | solution.py:32
  26.4 2.9 %collective-permute-start.2 = (bf16[128,768]{1,0:T(8,128)(2,1)}, bf16[128,768]{1,0:T(8,128)(2,1)}, u32[]{:S(2)}, u32[]{:S(2)}) collective-permute-start(bf16[128,768]{1,0:T(8,128)(2,1)} %get-tuple-element.35), channel_id=1, source_target_pairs={{0,32},{1,33},{2,34},{3,35},{4,36},{5,37},{6,38},{7,39},{8,40},{9,... | collective-permute-start | bytes 589832 | tf_op jit(solution)/shard_map/ppermute | solution.py:32
  29.6 3.3 %collective-permute-done.1 = bf16[128,768]{1,0:T(8,128)(2,1)S(1)} collective-permute-done((bf16[128,768]{1,0:T(8,128)(2,1)}, bf16[128,768]{1,0:T(8,128)(2,1)S(1)}, u32[]{:S(2)}, u32[]{:S(2)}) %collective-permute-start.1) | collective-permute-done | bytes 196640 | tf_op jit(solution)/shard_map/ppermute | solution.py:32
  32.8 6.1 %collective-permute-done.2 = bf16[128,768]{1,0:T(8,128)(2,1)} collective-permute-done((bf16[128,768]{1,0:T(8,128)(2,1)}, bf16[128,768]{1,0:T(8,128)(2,1)}, u32[]{:S(2)}, u32[]{:S(2)}) %collective-permute-start.2) | collective-permute-done | bytes 196640 | tf_op jit(solution)/shard_map/ppermute | solution.py:32
  38.9 2.4 %collective-permute-done.3 = bf16[128,768]{1,0:T(8,128)(2,1)} collective-permute-done((bf16[128,768]{1,0:T(8,128)(2,1)S(1)}, bf16[128,768]{1,0:T(8,128)(2,1)}, u32[]{:S(2)}, u32[]{:S(2)}) %collective-permute-start.3) | collective-permute-done | bytes 196640 | tf_op jit(solution)/shard_map/ppermute | solution.py:32
  41.3 1.2 fusion.9
  42.5 1.9 %collective-permute-start.4 = (bf16[32,768]{1,0:T(8,128)(2,1)S(1)}, bf16[32,768]{1,0:T(8,128)(2,1)S(1)}, u32[]{:S(2)}, u32[]{:S(2)}) collective-permute-start(bf16[32,768]{1,0:T(8,128)(2,1)S(1)} %get-tuple-element.39), channel_id=1, source_target_pairs={{0,4},{1,5},{2,6},{3,7},{4,0},{5,1},{6,2},{7,3},{8,12},{9,13},{10,... | collective-permute-start | bytes 147464 | tf_op jit(solution)/shard_map/ppermute | solution.py:32
  44.4 2.7 %collective-permute-start.5 = (bf16[32,768]{1,0:T(8,128)(2,1)S(1)}, bf16[32,768]{1,0:T(8,128)(2,1)S(1)}, u32[]{:S(2)}, u32[]{:S(2)}) collective-permute-start(bf16[32,768]{1,0:T(8,128)(2,1)S(1)} %get-tuple-element.41), channel_id=1, source_target_pairs={{0,8},{1,9},{2,10},{3,11},{4,12},{5,13},{6,14},{7,15},{8,0},{9,1},... | collective-permute-start | bytes 147464 | tf_op jit(solution)/shard_map/ppermute | solution.py:32
  47.3 1.2 constant_dynamic-slice_fusion.1.weight_ref
  48.5 1.7 %collective-permute-done.5 = bf16[32,768]{1,0:T(8,128)(2,1)S(1)} collective-permute-done((bf16[32,768]{1,0:T(8,128)(2,1)S(1)}, bf16[32,768]{1,0:T(8,128)(2,1)S(1)}, u32[]{:S(2)}, u32[]{:S(2)}) %collective-permute-start.5) | collective-permute-done | bytes 49184 | tf_op jit(solution)/shard_map/ppermute | solution.py:32
  50.1 2.3 %collective-permute-done.6 = bf16[32,768]{1,0:T(8,128)(2,1)S(1)} collective-permute-done((bf16[32,768]{1,0:T(8,128)(2,1)S(1)}, bf16[32,768]{1,0:T(8,128)(2,1)S(1)}, u32[]{:S(2)}, u32[]{:S(2)}) %collective-permute-start.6) | collective-permute-done | bytes 49184 | tf_op jit(solution)/shard_map/ppermute | solution.py:32
  52.4 0.7 collective-permute-start.7
  53.1 3.6 %collective-permute-start.8 = (bf16[32,768]{1,0:T(8,128)(2,1)S(1)}, bf16[32,768]{1,0:T(8,128)(2,1)S(1)}, u32[]{:S(2)}, u32[]{:S(2)}) collective-permute-start(bf16[32,768]{1,0:T(8,128)(2,1)S(1)} %fusion.30.a), channel_id=1, source_target_pairs={{0,2},{1,3},{2,0},{3,1},{4,6},{5,7},{6,4},{7,5},{8,10},{9,11},{10,... | collective-permute-start | bytes 147464 | tf_op jit(solution)/shard_map/ppermute | solution.py:32
  56.7 0.5 collective-permute-start.9
  57.2 2.9 %place_qkv.2.after.matrix_ref = bf16[3072,512]{1,0:T(8,128)(2,1)S(1)} custom-call(s32[7]{0:T(128)S(1)} %copy-done.12, bf16[512,2176]{1,0:T(8,128)(2,1)S(1)} %bitcast.70, bf16[768,512]{1,0:T(8,128)(2,1)S(1)} %constant_dynamic-slice_fusion.1.weight_ref), custom_call_target="tpu_custom_call" | custom-call | flops 1610612736 | bytes 6291456 | tf_op jit(solution)/shard_map/place_qkv/pallas_call | solution.py:50
  60.1 1.8 %collective-permute-done.9.d = bf16[32,768]{1,0:T(8,128)(2,1)S(1)} collective-permute-done((bf16[32,768]{1,0:T(8,128)(2,1)S(1)}, bf16[32,768]{1,0:T(8,128)(2,1)S(1)}, u32[]{:S(2)}, u32[]{:S(2)}) %collective-permute-start.9) | collective-permute-done | bytes 49184 | tf_op jit(solution)/shard_map/ppermute | solution.py:32
  62.2 2.0 %collective-permute-start.11 = (bf16[32,768]{1,0:T(8,128)(2,1)S(1)}, bf16[32,768]{1,0:T(8,128)(2,1)S(1)}, u32[]{:S(2)}, u32[]{:S(2)}) collective-permute-start(bf16[32,768]{1,0:T(8,128)(2,1)S(1)} %settle.1.refs_0_), channel_id=1, source_target_pairs={{0,8},{1,9},{2,10},{3,11},{4,12},{5,13},{6,14},{7,15},{8,0},{9,1},... | collective-permute-start | bytes 147464 | tf_op jit(solution)/shard_map/ppermute | solution.py:32
  64.2 2.7 %collective-permute-start.12 = (bf16[32,768]{1,0:T(8,128)(2,1)S(1)}, bf16[32,768]{1,0:T(8,128)(2,1)S(1)}, u32[]{:S(2)}, u32[]{:S(2)}) collective-permute-start(bf16[32,768]{1,0:T(8,128)(2,1)S(1)} %settle.1.refs_0_), channel_id=1, source_target_pairs={{0,12},{1,13},{2,14},{3,15},{4,8},{5,9},{6,10},{7,11},{8,4},{9,5},... | collective-permute-start | bytes 147464 | tf_op jit(solution)/shard_map/ppermute | solution.py:32
  66.9 1.6 %copy-done.3 = bf16[16,32,2176]{2,1,0:T(8,128)(2,1)S(1)} copy-done((bf16[16,32,2176]{2,1,0:T(8,128)(2,1)S(1)}, bf16[16,32,2176]{2,1,0:T(8,128)(2,1)}, u32[]{:S(2)}) %copy-start.3) | copy-done | bytes 2228248
  68.5 2.5 %place_qkv.3.refs_4_.matrix_ref = bf16[3072,512]{1,0:T(8,128)(2,1)S(1)} custom-call(s32[7]{0:T(128)S(1)} %copy-done.12, bf16[512,2176]{1,0:T(8,128)(2,1)S(1)} %bitcast.71, bf16[768,512]{1,0:T(8,128)(2,1)S(1)} %copy-done.7), custom_call_target="tpu_custom_call" | custom-call | flops 1610612736 | bytes 6291456 | tf_op jit(solution)/shard_map/place_qkv/pallas_call | solution.py:50
  71.2 1.7 %collective-permute-start.16 = (bf16[128,768]{1,0:T(8,128)(2,1)S(1)}, bf16[128,768]{1,0:T(8,128)(2,1)}, u32[]{:S(2)}, u32[]{:S(2)}) collective-permute-start(bf16[128,768]{1,0:T(8,128)(2,1)S(1)} %stack.33.p0), channel_id=1, source_target_pairs={{0,32},{1,33},{2,34},{3,35},{4,36},{5,37},{6,38},{7,39},{8,40},{9,... | collective-permute-start | bytes 589832 | tf_op jit(solution)/shard_map/ppermute | solution.py:32
  72.9 3.0 %collective-permute-start.18 = (bf16[128,768]{1,0:T(8,128)(2,1)S(1)}, bf16[128,768]{1,0:T(8,128)(2,1)}, u32[]{:S(2)}, u32[]{:S(2)}) collective-permute-start(bf16[128,768]{1,0:T(8,128)(2,1)S(1)} %stack.33.p0), channel_id=1, source_target_pairs={{0,48},{1,49},{2,50},{3,51},{4,52},{5,53},{6,54},{7,55},{8,56},{9,... | collective-permute-start | bytes 589832 | tf_op jit(solution)/shard_map/ppermute | solution.py:32
  75.9 1.9 %constant_dynamic-slice_fusion.weight_ref = bf16[48,6144]{1,0:T(8,128)(2,1)} fusion(bf16[384,6144]{1,0:T(8,128)(2,1)} %param.19, s32[]{:T(128)S(6)} %select_n.42), kind=kLoop, calls=%fused_computation.60 | loop fusion | bytes 1179652 | tf_op jit(solution)/shard_map/dynamic_slice | solution.py:530
  78.9 2.0 %collective-permute-done.18.p3 = bf16[128,768]{1,0:T(8,128)(2,1)} collective-permute-done((bf16[128,768]{1,0:T(8,128)(2,1)S(1)}, bf16[128,768]{1,0:T(8,128)(2,1)}, u32[]{:S(2)}, u32[]{:S(2)}) %collective-permute-start.18) | collective-permute-done | bytes 196640 | tf_op jit(solution)/shard_map/ppermute | solution.py:32
  81.0 1.9 %copy-done.1 = bf16[3072,512]{1,0:T(8,128)(2,1)S(1)} copy-done((bf16[3072,512]{1,0:T(8,128)(2,1)S(1)}, bf16[3072,512]{1,0:T(8,128)(2,1)}, u32[]{:S(2)}) %copy-start.1) | copy-done | bytes 3145752
  82.9 2.3 %project_first.1 = (f32[128,512]{1,0:T(8,128)S(1)}, f32[128,128]{1,0:T(8,128)S(1)}) custom-call(s32[7]{0:T(128)S(1)} %copy-done.12, bf16[128,768]{1,0:T(8,128)(2,1)S(1)} %stack.33.p0, bf16[128,768]{1,0:T(8,128)(2,1)S(1)} %collective-permute-done.14.p1, bf16[128,768]{1,0:T(8,128)(2,1)} %collective-permute-done.16.p2, ...), custom_call_target="tpu_custom_call" | custom-call | flops 402653184 | bytes 4194304 | tf_op jit(solution)/shard_map/project_first/pallas_call | solution.py:50
  85.3 2.7 %project_last.1 = (bf16[32,512]{1,0:T(8,128)(2,1)S(1)}, bf16[32,512]{1,0:T(8,128)(2,1)S(1)}, bf16[32,512]{1,0:T(8,128)(2,1)S(1)}, bf16[32,512]{1,0:T(8,128)(2,1)S(1)}) custom-call(s32[7]{0:T(128)S(1)} %copy-done.12, bf16[128,768]{1,0:T(8,128)(2,1)} %collective-permute-done.13.p0, bf16[128,768]{1,0:T(8,128)(2,1)} %collective-permute-done.15.p1, ...), custom_call_target="tpu_custom_call" | custom-call | flops 402653184 | bytes 4194304 | tf_op jit(solution)/shard_map/project_last/pallas_call | solution.py:50
  88.3 4.2 %collective-permute-start.21 = (bf16[32,512]{1,0:T(8,128)(2,1)S(1)}, bf16[32,512]{1,0:T(8,128)(2,1)S(1)}, u32[]{:S(2)}, u32[]{:S(2)}) collective-permute-start(bf16[32,512]{1,0:T(8,128)(2,1)S(1)} %get-tuple-element.21), channel_id=1, source_target_pairs={{0,32},{1,33},{2,34},{3,35},{4,36},{5,37},{6,38},{7,39},{8,40},{9,... | collective-permute-start | bytes 98312 | tf_op jit(solution)/shard_map/ppermute | solution.py:32
  92.9 2.1 %collective-permute-done.21.c = bf16[32,512]{1,0:T(8,128)(2,1)S(1)} collective-permute-done((bf16[32,512]{1,0:T(8,128)(2,1)S(1)}, bf16[32,512]{1,0:T(8,128)(2,1)S(1)}, u32[]{:S(2)}, u32[]{:S(2)}) %collective-permute-start.21) | collective-permute-done | bytes 32800 | tf_op jit(solution)/shard_map/ppermute | solution.py:32
  95.0 2.6 %collective-permute-done.22.d = bf16[32,512]{1,0:T(8,128)(2,1)S(1)} collective-permute-done((bf16[32,512]{1,0:T(8,128)(2,1)S(1)}, bf16[32,512]{1,0:T(8,128)(2,1)S(1)}, u32[]{:S(2)}, u32[]{:S(2)}) %collective-permute-start.22) | collective-permute-done | bytes 32800 | tf_op jit(solution)/shard_map/ppermute | solution.py:32
  97.8 2.0 %collective-permute-start.25 = (bf16[8,512]{1,0:T(8,128)(2,1)S(1)}, bf16[8,512]{1,0:T(8,128)(2,1)S(1)}, u32[]{:S(2)}, u32[]{:S(2)}) collective-permute-start(bf16[8,512]{1,0:T(8,128)(2,1)S(1)} %get-tuple-element.26), channel_id=1, source_target_pairs={{0,65},{1,64},{2,67},{3,66},{4,69},{5,68},{6,71},{7,70},{8,73},{9,... | collective-permute-start | bytes 24584 | tf_op jit(solution)/shard_map/ppermute | solution.py:32
  99.9 1.4 collective-permute-done.23.own1
  101.4 2.0 %attend.1 = (bf16[8,384]{1,0:T(8,128)(2,1)S(1)}, bf16[8,384]{1,0:T(8,128)(2,1)S(1)}) custom-call(s32[7]{0:T(128)S(1)} %copy-done.12, s32[4]{0:T(128)S(1)} %copy-done.13, bf16[8,512]{1,0:T(8,128)(2,1)S(1)} %get-tuple-element.23.own0, bf16[8,512]{1,0:T(8,128)(2,1)S(1)} %collective-permute-done.23.own1, bf16[8,512]{1,0:T(8,128)(2,1)S(1)} %collective-permute-done.24.other0, ...), custom_call_target="tpu_custom_call" | custom-call | flops 201326592 | bytes 5242880 | tf_op jit(solution)/shard_map/attend/pallas_call | solution.py:50
  103.6 1.5 collective-permute-start.28
  105.6 3.5 %place_out.1.after.matrix_ref = bf16[384,6144]{1,0:T(8,128)(2,1)S(1)} custom-call(s32[7]{0:T(128)S(1)} %copy-done.12, bf16[512,2176]{1,0:T(8,128)(2,1)S(1)} %bitcast.72, bf16[48,6144]{1,0:T(8,128)(2,1)S(1)} %copy-done.10), custom_call_target="tpu_custom_call" | custom-call | flops 2415919104 | bytes 7340032 | tf_op jit(solution)/shard_map/place_out/pallas_call | solution.py:50
  109.2 0.6 heads.1.a0
  109.9 1.7 %collective-permute-start.30 = (bf16[32,384]{1,0:T(8,128)(2,1)S(1)}, bf16[32,384]{1,0:T(8,128)(2,1)S(1)}, u32[]{:S(2)}, u32[]{:S(2)}) collective-permute-start(bf16[32,384]{1,0:T(8,128)(2,1)S(1)} %heads.1.a0), channel_id=1, source_target_pairs={{0,32},{1,33},{2,34},{3,35},{4,36},{5,37},{6,38},{7,39},{8,40},{9,... | collective-permute-start | bytes 73736 | tf_op jit(solution)/shard_map/ppermute | solution.py:32
  111.6 3.0 %collective-permute-start.31 = (bf16[32,384]{1,0:T(8,128)(2,1)S(1)}, bf16[32,384]{1,0:T(8,128)(2,1)S(1)}, u32[]{:S(2)}, u32[]{:S(2)}) collective-permute-start(bf16[32,384]{1,0:T(8,128)(2,1)S(1)} %heads.1.a0), channel_id=1, source_target_pairs={{0,48},{1,49},{2,50},{3,51},{4,52},{5,53},{6,54},{7,55},{8,56},{9,... | collective-permute-start | bytes 73736 | tf_op jit(solution)/shard_map/ppermute | solution.py:32
  114.6 0.7 collective-permute-done.30.a2
  115.3 1.3 collective-permute-done.31.a3
  116.7 2.8 %share.3 = bf16[4,4,2,32,384]{4,3,2,1,0:T(8,128)(2,1)S(1)} custom-call(s32[7]{0:T(128)S(1)} %copy-done.12, bf16[32,384]{1,0:T(8,128)(2,1)S(1)} %heads.1.a0, bf16[32,384]{1,0:T(8,128)(2,1)S(1)} %collective-permute-done.29.a1, bf16[32,384]{1,0:T(8,128)(2,1)S(1)} %collective-permute-done.30.a2, bf16[32,384]{1,0:T(8,128)(2,1)S(1)} %collective-permute-done.31.a3, ...), custom_call_target="tpu_custom_call" | custom-call | flops 301989888 | bytes 4194304 | tf_op jit(solution)/shard_map/share/pallas_call | solution.py:50
  119.8 2.8 %share.2 = bf16[4,4,2,32,384]{4,3,2,1,0:T(8,128)(2,1)S(1)} custom-call(s32[7]{0:T(128)S(1)} %copy-done.12, bf16[32,384]{1,0:T(8,128)(2,1)S(1)} %heads.1.a0, bf16[32,384]{1,0:T(8,128)(2,1)S(1)} %collective-permute-done.29.a1, bf16[32,384]{1,0:T(8,128)(2,1)S(1)} %collective-permute-done.30.a2, bf16[32,384]{1,0:T(8,128)(2,1)S(1)} %collective-permute-done.31.a3, ...), custom_call_target="tpu_custom_call" | custom-call | flops 301989888 | bytes 4194304 | tf_op jit(solution)/shard_map/share/pallas_call | solution.py:50
  122.9 2.6 %collective-permute-start.34 = (bf16[4,2,32,384]{3,2,1,0:T(8,128)(2,1)S(1)}, bf16[4,2,32,384]{3,2,1,0:T(8,128)(2,1)S(1)}, u32[]{:S(2)}, u32[]{:S(2)}) collective-permute-start(bf16[4,2,32,384]{3,2,1,0:T(8,128)(2,1)S(1)} %get-tuple-element.31), channel_id=1, source_target_pairs={{0,8},{1,9},{2,10},{3,11},{4,12},{5,13},{6,14},{7,15},{8,0},{9,1},... | collective-permute-start | bytes 589832 | tf_op jit(solution)/shard_map/ppermute | solution.py:32
  125.5 2.1 %collective-permute-start.35 = (bf16[4,2,32,384]{3,2,1,0:T(8,128)(2,1)S(1)}, bf16[4,2,32,384]{3,2,1,0:T(8,128)(2,1)S(1)}, u32[]{:S(2)}, u32[]{:S(2)}) collective-permute-start(bf16[4,2,32,384]{3,2,1,0:T(8,128)(2,1)S(1)} %get-tuple-element.30), channel_id=1, source_target_pairs={{0,12},{1,13},{2,14},{3,15},{4,8},{5,9},{6,10},{7,11},{8,4},{9,5},... | collective-permute-start | bytes 589832 | tf_op jit(solution)/shard_map/ppermute | solution.py:32
  127.6 3.0 %collective-permute-done.33 = bf16[4,2,32,384]{3,2,1,0:T(8,128)(2,1)S(1)} collective-permute-done((bf16[4,2,32,384]{3,2,1,0:T(8,128)(2,1)S(1)}, bf16[4,2,32,384]{3,2,1,0:T(8,128)(2,1)S(1)}, u32[]{:S(2)}, u32[]{:S(2)}) %collective-permute-start.33) | collective-permute-done | bytes 196640 | tf_op jit(solution)/shard_map/ppermute | solution.py:32
  130.6 4.5 %collective-permute-done.34 = bf16[4,2,32,384]{3,2,1,0:T(8,128)(2,1)S(1)} collective-permute-done((bf16[4,2,32,384]{3,2,1,0:T(8,128)(2,1)S(1)}, bf16[4,2,32,384]{3,2,1,0:T(8,128)(2,1)S(1)}, u32[]{:S(2)}, u32[]{:S(2)}) %collective-permute-start.34) | collective-permute-done | bytes 196640 | tf_op jit(solution)/shard_map/ppermute | solution.py:32
  135.1 2.6 %collective-permute-done.35 = bf16[4,2,32,384]{3,2,1,0:T(8,128)(2,1)S(1)} collective-permute-done((bf16[4,2,32,384]{3,2,1,0:T(8,128)(2,1)S(1)}, bf16[4,2,32,384]{3,2,1,0:T(8,128)(2,1)S(1)}, u32[]{:S(2)}, u32[]{:S(2)}) %collective-permute-start.35) | collective-permute-done | bytes 196640 | tf_op jit(solution)/shard_map/ppermute | solution.py:32
  137.8 0.7 collective-permute-start.36
  138.4 3.8 %collective-permute-start.37 = (bf16[2,32,384]{2,1,0:T(8,128)(2,1)S(1)}, bf16[2,32,384]{2,1,0:T(8,128)(2,1)S(1)}, u32[]{:S(2)}, u32[]{:S(2)}) collective-permute-start(bf16[2,32,384]{2,1,0:T(8,128)(2,1)S(1)} %get-tuple-element.38), channel_id=1, source_target_pairs={{0,32},{1,33},{2,34},{3,35},{4,36},{5,37},{6,38},{7,39},{8,40},{9,... | collective-permute-start | bytes 147464 | tf_op jit(solution)/shard_map/ppermute | solution.py:32
  142.6 2.3 %collective-permute-done.37 = bf16[2,32,384]{2,1,0:T(8,128)(2,1)S(1)} collective-permute-done((bf16[2,32,384]{2,1,0:T(8,128)(2,1)S(1)}, bf16[2,32,384]{2,1,0:T(8,128)(2,1)S(1)}, u32[]{:S(2)}, u32[]{:S(2)}) %collective-permute-start.37) | collective-permute-done | bytes 49184 | tf_op jit(solution)/shard_map/ppermute | solution.py:32
  144.9 2.7 %collective-permute-done.38 = bf16[2,32,384]{2,1,0:T(8,128)(2,1)S(1)} collective-permute-done((bf16[2,32,384]{2,1,0:T(8,128)(2,1)S(1)}, bf16[2,32,384]{2,1,0:T(8,128)(2,1)S(1)}, u32[]{:S(2)}, u32[]{:S(2)}) %collective-permute-start.38) | collective-permute-done | bytes 49184 | tf_op jit(solution)/shard_map/ppermute | solution.py:32
  147.6 1.6 %collective-permute-start.39 = (bf16[16,384]{1,0:T(8,128)(2,1)S(1)}, bf16[16,384]{1,0:T(8,128)(2,1)S(1)}, u32[]{:S(2)}, u32[]{:S(2)}) collective-permute-start(bf16[16,384]{1,0:T(8,128)(2,1)S(1)} %get-tuple-element.44), channel_id=1, source_target_pairs={{0,64},{1,65},{2,66},{3,67},{4,68},{5,69},{6,70},{7,71},{8,72},{9,... | collective-permute-start | bytes 36872 | tf_op jit(solution)/shard_map/ppermute | solution.py:32
  149.7 2.7 %collective-permute-start.41 = (bf16[16,384]{1,0:T(8,128)(2,1)S(1)}, bf16[16,384]{1,0:T(8,128)(2,1)S(1)}, u32[]{:S(2)}, u32[]{:S(2)}) collective-permute-start(bf16[16,384]{1,0:T(8,128)(2,1)S(1)} %get-tuple-element.42), channel_id=1, source_target_pairs={{0,66},{1,67},{2,64},{3,65},{4,70},{5,71},{6,68},{7,69},{8,74},{9,... | collective-permute-start | bytes 36872 | tf_op jit(solution)/shard_map/ppermute | solution.py:32
  152.4 2.0 %collective-permute-done.40.c = bf16[16,384]{1,0:T(8,128)(2,1)S(1)} collective-permute-done((bf16[16,384]{1,0:T(8,128)(2,1)S(1)}, bf16[16,384]{1,0:T(8,128)(2,1)S(1)}, u32[]{:S(2)}, u32[]{:S(2)}) %collective-permute-start.40) | collective-permute-done | bytes 12320 | tf_op jit(solution)/shard_map/ppermute | solution.py:32
  154.6 0.6 finish.1
  (88 shorter events, 6.0 us)
Async XLA Ops:
  6.5 8.1 %copy-start.15 = (s32[32,4]{0,1:T(4,128)S(1)}, s32[32,4]{0,1:T(4,128)}, u32[]{:S(2)}) copy-start(s32[32,4]{0,1:T(4,128)} %param.14) | copy-start | bytes 1540
  6.5 50.7 %all-to-all-start = ((bf16[16,32,2176]{2,1,0:T(8,128)(2,1)}), bf16[16,32,2176]{2,1,0:T(8,128)(2,1)S(1)}, u32[]{:S(2)}, u32[]{:S(2)}) async-start(bf16[16,32,2176]{2,1,0:T(8,128)(2,1)} %bitcast.73), calls=%async_computation | async-start | bytes 4456448 | tf_op jit(solution)/shard_map/all_to_all | solution.py:528
  15.2 4.8 %copy-start.11 = (s32[32,4]{1,0:T(8,128)S(1)}, s32[32,4]{1,0:T(8,128)}, u32[]{:S(2)}) copy-start(s32[32,4]{1,0:T(8,128)} %copy.16.ids_ref) | copy-start | bytes 1540
  15.9 4.2 %copy-start.5 = (bf16[256,6144]{1,0:T(8,128)(2,1)S(1)}, bf16[256,6144]{1,0:T(8,128)(2,1)}, u32[]{:S(2)}) copy-start(bf16[256,6144]{1,0:T(8,128)(2,1)} %embed_ref.3) | copy-start | bytes 9437188
  15.9 4.2 %copy-start.12 = (s32[7]{0:T(128)S(1)}, s32[7]{0:T(128)}, u32[]{:S(2)}) copy-start(s32[7]{0:T(128)} %stack.32.pos) | copy-start | bytes 88
  19.7 3.5 %collective-permute-start = (bf16[4,128,768]{2,1,0:T(8,128)(2,1)}, bf16[4,128,768]{2,1,0:T(8,128)(2,1)S(1)}, u32[]{:S(2)}, u32[]{:S(2)}) collective-permute-start(bf16[4,128,768]{2,1,0:T(8,128)(2,1)} %embed_part.2.after), channel_id=1, source_target_pairs={{0,1},{1,0},{2,3},{3,2},{4,5},{5,4},{6,7},{7,6},{8,9},{9,8},{10,11... | collective-permute-start | bytes 2359304 | tf_op jit(solution)/shard_map/ppermute | solution.py:32
  20.1 1.1 copy-start.9
  23.1 0.9 copy-start.14
  24.9 8.0 %collective-permute-start.1 = (bf16[128,768]{1,0:T(8,128)(2,1)}, bf16[128,768]{1,0:T(8,128)(2,1)S(1)}, u32[]{:S(2)}, u32[]{:S(2)}) collective-permute-start(bf16[128,768]{1,0:T(8,128)(2,1)} %get-tuple-element.33), channel_id=1, source_target_pairs={{0,16},{1,17},{2,18},{3,19},{4,20},{5,21},{6,22},{7,23},{8,24},{9,... | collective-permute-start | bytes 589832 | tf_op jit(solution)/shard_map/ppermute | solution.py:32
  26.4 12.5 %collective-permute-start.2 = (bf16[128,768]{1,0:T(8,128)(2,1)}, bf16[128,768]{1,0:T(8,128)(2,1)}, u32[]{:S(2)}, u32[]{:S(2)}) collective-permute-start(bf16[128,768]{1,0:T(8,128)(2,1)} %get-tuple-element.35), channel_id=1, source_target_pairs={{0,32},{1,33},{2,34},{3,35},{4,36},{5,37},{6,38},{7,39},{8,40},{9,... | collective-permute-start | bytes 589832 | tf_op jit(solution)/shard_map/ppermute | solution.py:32
  29.3 11.9 %collective-permute-start.3 = (bf16[128,768]{1,0:T(8,128)(2,1)S(1)}, bf16[128,768]{1,0:T(8,128)(2,1)}, u32[]{:S(2)}, u32[]{:S(2)}) collective-permute-start(bf16[128,768]{1,0:T(8,128)(2,1)S(1)} %get-tuple-element.34), channel_id=1, source_target_pairs={{0,48},{1,49},{2,50},{3,51},{4,52},{5,53},{6,54},{7,55},{8,56},{9,... | collective-permute-start | bytes 589832 | tf_op jit(solution)/shard_map/ppermute | solution.py:32
  42.5 6.0 %collective-permute-start.4 = (bf16[32,768]{1,0:T(8,128)(2,1)S(1)}, bf16[32,768]{1,0:T(8,128)(2,1)S(1)}, u32[]{:S(2)}, u32[]{:S(2)}) collective-permute-start(bf16[32,768]{1,0:T(8,128)(2,1)S(1)} %get-tuple-element.39), channel_id=1, source_target_pairs={{0,4},{1,5},{2,6},{3,7},{4,0},{5,1},{6,2},{7,3},{8,12},{9,13},{10,... | collective-permute-start | bytes 147464 | tf_op jit(solution)/shard_map/ppermute | solution.py:32
  44.4 5.7 %collective-permute-start.5 = (bf16[32,768]{1,0:T(8,128)(2,1)S(1)}, bf16[32,768]{1,0:T(8,128)(2,1)S(1)}, u32[]{:S(2)}, u32[]{:S(2)}) collective-permute-start(bf16[32,768]{1,0:T(8,128)(2,1)S(1)} %get-tuple-element.41), channel_id=1, source_target_pairs={{0,8},{1,9},{2,10},{3,11},{4,12},{5,13},{6,14},{7,15},{8,0},{9,1},... | collective-permute-start | bytes 147464 | tf_op jit(solution)/shard_map/ppermute | solution.py:32
  47.1 5.3 %collective-permute-start.6 = (bf16[32,768]{1,0:T(8,128)(2,1)S(1)}, bf16[32,768]{1,0:T(8,128)(2,1)S(1)}, u32[]{:S(2)}, u32[]{:S(2)}) collective-permute-start(bf16[32,768]{1,0:T(8,128)(2,1)S(1)} %get-tuple-element.40), channel_id=1, source_target_pairs={{0,12},{1,13},{2,14},{3,15},{4,8},{5,9},{6,10},{7,11},{8,4},{9,5},... | collective-permute-start | bytes 147464 | tf_op jit(solution)/shard_map/ppermute | solution.py:32
  48.4 11.6 %copy-start.6 = (bf16[768,512]{1,0:T(8,128)(2,1)}, bf16[768,512]{1,0:T(8,128)(2,1)S(1)}, u32[]{:S(2)}) copy-start(bf16[768,512]{1,0:T(8,128)(2,1)S(1)} %constant_dynamic-slice_fusion.1.weight_ref) | copy-start | bytes 2359300
  52.4 7.7 %collective-permute-start.7 = (bf16[32,768]{1,0:T(8,128)(2,1)S(1)}, bf16[32,768]{1,0:T(8,128)(2,1)S(1)}, u32[]{:S(2)}, u32[]{:S(2)}) collective-permute-start(bf16[32,768]{1,0:T(8,128)(2,1)S(1)} %fusion.30.a), channel_id=1, source_target_pairs={{0,64},{1,65},{2,66},{3,67},{4,68},{5,69},{6,70},{7,71},{8,72},{9,... | collective-permute-start | bytes 147464 | tf_op jit(solution)/shard_map/ppermute | solution.py:32
  53.1 7.0 %collective-permute-start.8 = (bf16[32,768]{1,0:T(8,128)(2,1)S(1)}, bf16[32,768]{1,0:T(8,128)(2,1)S(1)}, u32[]{:S(2)}, u32[]{:S(2)}) collective-permute-start(bf16[32,768]{1,0:T(8,128)(2,1)S(1)} %fusion.30.a), channel_id=1, source_target_pairs={{0,2},{1,3},{2,0},{3,1},{4,6},{5,7},{6,4},{7,5},{8,10},{9,11},{10,... | collective-permute-start | bytes 147464 | tf_op jit(solution)/shard_map/ppermute | solution.py:32
  56.7 5.3 %collective-permute-start.9 = (bf16[32,768]{1,0:T(8,128)(2,1)S(1)}, bf16[32,768]{1,0:T(8,128)(2,1)S(1)}, u32[]{:S(2)}, u32[]{:S(2)}) collective-permute-start(bf16[32,768]{1,0:T(8,128)(2,1)S(1)} %fusion.30.a), channel_id=1, source_target_pairs={{0,66},{1,67},{2,64},{3,65},{4,70},{5,71},{6,68},{7,69},{8,74},{9,... | collective-permute-start | bytes 147464 | tf_op jit(solution)/shard_map/ppermute | solution.py:32
  57.2 5.0 %copy-start.2 = (bf16[16,32,2176]{2,1,0:T(8,128)(2,1)}, bf16[16,32,2176]{2,1,0:T(8,128)(2,1)S(1)}, u32[]{:S(2)}) copy-start(bf16[16,32,2176]{2,1,0:T(8,128)(2,1)S(1)} %all-to-all-done) | copy-start | bytes 6684676
  60.1 10.9 %copy-start = (bf16[3072,512]{1,0:T(8,128)(2,1)}, bf16[3072,512]{1,0:T(8,128)(2,1)S(1)}, u32[]{:S(2)}) copy-start(bf16[3072,512]{1,0:T(8,128)(2,1)S(1)} %place_qkv.2.after.matrix_ref) | copy-start | bytes 9437188
  60.1 6.8 %copy-start.7 = (bf16[768,512]{1,0:T(8,128)(2,1)S(1)}, bf16[768,512]{1,0:T(8,128)(2,1)}, u32[]{:S(2)}) copy-start(bf16[768,512]{1,0:T(8,128)(2,1)} %copy-done.6) | copy-start | bytes 2359300
  62.2 8.9 %collective-permute-start.10 = (bf16[32,768]{1,0:T(8,128)(2,1)S(1)}, bf16[32,768]{1,0:T(8,128)(2,1)S(1)}, u32[]{:S(2)}, u32[]{:S(2)}) collective-permute-start(bf16[32,768]{1,0:T(8,128)(2,1)S(1)} %settle.1.refs_0_), channel_id=1, source_target_pairs={{0,4},{1,5},{2,6},{3,7},{4,0},{5,1},{6,2},{7,3},{8,12},{9,13},{10,... | collective-permute-start | bytes 147464 | tf_op jit(solution)/shard_map/ppermute | solution.py:32
  62.2 8.8 %collective-permute-start.11 = (bf16[32,768]{1,0:T(8,128)(2,1)S(1)}, bf16[32,768]{1,0:T(8,128)(2,1)S(1)}, u32[]{:S(2)}, u32[]{:S(2)}) collective-permute-start(bf16[32,768]{1,0:T(8,128)(2,1)S(1)} %settle.1.refs_0_), channel_id=1, source_target_pairs={{0,8},{1,9},{2,10},{3,11},{4,12},{5,13},{6,14},{7,15},{8,0},{9,1},... | collective-permute-start | bytes 147464 | tf_op jit(solution)/shard_map/ppermute | solution.py:32
  64.2 6.8 %collective-permute-start.12 = (bf16[32,768]{1,0:T(8,128)(2,1)S(1)}, bf16[32,768]{1,0:T(8,128)(2,1)S(1)}, u32[]{:S(2)}, u32[]{:S(2)}) collective-permute-start(bf16[32,768]{1,0:T(8,128)(2,1)S(1)} %settle.1.refs_0_), channel_id=1, source_target_pairs={{0,12},{1,13},{2,14},{3,15},{4,8},{5,9},{6,10},{7,11},{8,4},{9,5},... | collective-permute-start | bytes 147464 | tf_op jit(solution)/shard_map/ppermute | solution.py:32
  66.9 1.6 %copy-start.3 = (bf16[16,32,2176]{2,1,0:T(8,128)(2,1)S(1)}, bf16[16,32,2176]{2,1,0:T(8,128)(2,1)}, u32[]{:S(2)}) copy-start(bf16[16,32,2176]{2,1,0:T(8,128)(2,1)} %copy-done.2) | copy-start | bytes 6684676
  71.0 6.8 %copy-start.13 = (s32[4]{0:T(128)S(1)}, s32[4]{0:T(128)}, u32[]{:S(2)}) copy-start(s32[4]{0:T(128)} %lengths.1) | copy-start | bytes 52
  71.1 6.8 %collective-permute-start.14 = (bf16[128,768]{1,0:T(8,128)(2,1)S(1)}, bf16[128,768]{1,0:T(8,128)(2,1)S(1)}, u32[]{:S(2)}, u32[]{:S(2)}) collective-permute-start(bf16[128,768]{1,0:T(8,128)(2,1)S(1)} %stack.33.p0), channel_id=1, source_target_pairs={{0,16},{1,17},{2,18},{3,19},{4,20},{5,21},{6,22},{7,23},{8,24},{9,... | collective-permute-start | bytes 589832 | tf_op jit(solution)/shard_map/ppermute | solution.py:32
  71.2 7.7 %collective-permute-start.16 = (bf16[128,768]{1,0:T(8,128)(2,1)S(1)}, bf16[128,768]{1,0:T(8,128)(2,1)}, u32[]{:S(2)}, u32[]{:S(2)}) collective-permute-start(bf16[128,768]{1,0:T(8,128)(2,1)S(1)} %stack.33.p0), channel_id=1, source_target_pairs={{0,32},{1,33},{2,34},{3,35},{4,36},{5,37},{6,38},{7,39},{8,40},{9,... | collective-permute-start | bytes 589832 | tf_op jit(solution)/shard_map/ppermute | solution.py:32
  72.9 8.0 %collective-permute-start.18 = (bf16[128,768]{1,0:T(8,128)(2,1)S(1)}, bf16[128,768]{1,0:T(8,128)(2,1)}, u32[]{:S(2)}, u32[]{:S(2)}) collective-permute-start(bf16[128,768]{1,0:T(8,128)(2,1)S(1)} %stack.33.p0), channel_id=1, source_target_pairs={{0,48},{1,49},{2,50},{3,51},{4,52},{5,53},{6,54},{7,55},{8,56},{9,... | collective-permute-start | bytes 589832 | tf_op jit(solution)/shard_map/ppermute | solution.py:32
  77.9 7.4 %collective-permute-start.13 = (bf16[128,768]{1,0:T(8,128)(2,1)S(1)}, bf16[128,768]{1,0:T(8,128)(2,1)}, u32[]{:S(2)}, u32[]{:S(2)}) collective-permute-start(bf16[128,768]{1,0:T(8,128)(2,1)S(1)} %stack.33.p0), channel_id=1, source_target_pairs={{0,1},{1,0},{2,3},{3,2},{4,5},{5,4},{6,7},{7,6},{8,9},{9,8},{10,11... | collective-permute-start | bytes 589832 | tf_op jit(solution)/shard_map/ppermute | solution.py:32
  77.9 7.4 %collective-permute-start.15 = (bf16[128,768]{1,0:T(8,128)(2,1)S(1)}, bf16[128,768]{1,0:T(8,128)(2,1)}, u32[]{:S(2)}, u32[]{:S(2)}) collective-permute-start(bf16[128,768]{1,0:T(8,128)(2,1)S(1)} %collective-permute-done.14.p1), channel_id=1, source_target_pairs={{0,1},{1,0},{2,3},{3,2},{4,5},{5,4},{6,7},{7,6},{8,9},{9,8},{10,11... | collective-permute-start | bytes 589832 | tf_op jit(solution)/shard_map/ppermute | solution.py:32
  78.9 6.4 %collective-permute-start.17 = (bf16[128,768]{1,0:T(8,128)(2,1)}, bf16[128,768]{1,0:T(8,128)(2,1)}, u32[]{:S(2)}, u32[]{:S(2)}) collective-permute-start(bf16[128,768]{1,0:T(8,128)(2,1)} %collective-permute-done.16.p2), channel_id=1, source_target_pairs={{0,1},{1,0},{2,3},{3,2},{4,5},{5,4},{6,7},{7,6},{8,9},{9,8},{10,11... | collective-permute-start | bytes 589832 | tf_op jit(solution)/shard_map/ppermute | solution.py:32
  80.9 4.4 %collective-permute-start.19 = (bf16[128,768]{1,0:T(8,128)(2,1)}, bf16[128,768]{1,0:T(8,128)(2,1)}, u32[]{:S(2)}, u32[]{:S(2)}) collective-permute-start(bf16[128,768]{1,0:T(8,128)(2,1)} %collective-permute-done.18.p3), channel_id=1, source_target_pairs={{0,1},{1,0},{2,3},{3,2},{4,5},{5,4},{6,7},{7,6},{8,9},{9,8},{10,11... | collective-permute-start | bytes 589832 | tf_op jit(solution)/shard_map/ppermute | solution.py:32
  81.0 1.9 %copy-start.1 = (bf16[3072,512]{1,0:T(8,128)(2,1)S(1)}, bf16[3072,512]{1,0:T(8,128)(2,1)}, u32[]{:S(2)}) copy-start(bf16[3072,512]{1,0:T(8,128)(2,1)} %copy-done) | copy-start | bytes 9437188
  85.2 16.1 %copy-start.8 = (bf16[1,2,4096,256]{3,2,1,0:T(8,128)(2,1)S(1)}, bf16[1,2,4096,256]{3,2,1,0:T(8,128)(2,1)}, u32[]{:S(2)}) copy-start(bf16[1,2,4096,256]{3,2,1,0:T(8,128)(2,1)} %cache.1) | copy-start | bytes 12582916
  88.0 17.7 %copy-start.4 = (bf16[16,32,2176]{2,1,0:T(8,128)(2,1)S(1)}, bf16[16,32,2176]{2,1,0:T(8,128)(2,1)}, u32[]{:S(2)}) copy-start(bf16[16,32,2176]{2,1,0:T(8,128)(2,1)} %copy-done.2) | copy-start | bytes 6684676
  88.0 17.7 %copy-start.10 = (bf16[48,6144]{1,0:T(8,128)(2,1)S(1)}, bf16[48,6144]{1,0:T(8,128)(2,1)}, u32[]{:S(2)}) copy-start(bf16[48,6144]{1,0:T(8,128)(2,1)} %constant_dynamic-slice_fusion.weight_ref) | copy-start | bytes 1769476
  88.0 4.9 %collective-permute-start.20 = (bf16[32,512]{1,0:T(8,128)(2,1)S(1)}, bf16[32,512]{1,0:T(8,128)(2,1)S(1)}, u32[]{:S(2)}, u32[]{:S(2)}) collective-permute-start(bf16[32,512]{1,0:T(8,128)(2,1)S(1)} %get-tuple-element.20), channel_id=1, source_target_pairs={{0,16},{1,17},{2,18},{3,19},{4,20},{5,21},{6,22},{7,23},{8,24},{9,... | collective-permute-start | bytes 98312 | tf_op jit(solution)/shard_map/ppermute | solution.py:32
  88.3 6.7 %collective-permute-start.21 = (bf16[32,512]{1,0:T(8,128)(2,1)S(1)}, bf16[32,512]{1,0:T(8,128)(2,1)S(1)}, u32[]{:S(2)}, u32[]{:S(2)}) collective-permute-start(bf16[32,512]{1,0:T(8,128)(2,1)S(1)} %get-tuple-element.21), channel_id=1, source_target_pairs={{0,32},{1,33},{2,34},{3,35},{4,36},{5,37},{6,38},{7,39},{8,40},{9,... | collective-permute-start | bytes 98312 | tf_op jit(solution)/shard_map/ppermute | solution.py:32
  92.5 5.1 %collective-permute-start.22 = (bf16[32,512]{1,0:T(8,128)(2,1)S(1)}, bf16[32,512]{1,0:T(8,128)(2,1)S(1)}, u32[]{:S(2)}, u32[]{:S(2)}) collective-permute-start(bf16[32,512]{1,0:T(8,128)(2,1)S(1)} %get-tuple-element.22), channel_id=1, source_target_pairs={{0,48},{1,49},{2,50},{3,51},{4,52},{5,53},{6,54},{7,55},{8,56},{9,... | collective-permute-start | bytes 98312 | tf_op jit(solution)/shard_map/ppermute | solution.py:32
  97.6 3.7 %collective-permute-start.23 = (bf16[8,512]{1,0:T(8,128)(2,1)S(1)}, bf16[8,512]{1,0:T(8,128)(2,1)S(1)}, u32[]{:S(2)}, u32[]{:S(2)}) collective-permute-start(bf16[8,512]{1,0:T(8,128)(2,1)S(1)} %get-tuple-element.24), channel_id=1, source_target_pairs={{0,64},{1,65},{2,66},{3,67},{4,68},{5,69},{6,70},{7,71},{8,72},{9,... | collective-permute-start | bytes 24584 | tf_op jit(solution)/shard_map/ppermute | solution.py:32
  97.7 3.6 %collective-permute-start.24 = (bf16[8,512]{1,0:T(8,128)(2,1)S(1)}, bf16[8,512]{1,0:T(8,128)(2,1)S(1)}, u32[]{:S(2)}, u32[]{:S(2)}) collective-permute-start(bf16[8,512]{1,0:T(8,128)(2,1)S(1)} %get-tuple-element.25), channel_id=1, source_target_pairs={{0,1},{1,0},{2,3},{3,2},{4,5},{5,4},{6,7},{7,6},{8,9},{9,8},{10,11... | collective-permute-start | bytes 24584 | tf_op jit(solution)/shard_map/ppermute | solution.py:32
  97.8 3.6 %collective-permute-start.25 = (bf16[8,512]{1,0:T(8,128)(2,1)S(1)}, bf16[8,512]{1,0:T(8,128)(2,1)S(1)}, u32[]{:S(2)}, u32[]{:S(2)}) collective-permute-start(bf16[8,512]{1,0:T(8,128)(2,1)S(1)} %get-tuple-element.26), channel_id=1, source_target_pairs={{0,65},{1,64},{2,67},{3,66},{4,69},{5,68},{6,71},{7,70},{8,73},{9,... | collective-permute-start | bytes 24584 | tf_op jit(solution)/shard_map/ppermute | solution.py:32
  103.4 5.8 %collective-permute-start.26 = (bf16[8,384]{1,0:T(8,128)(2,1)S(1)}, bf16[8,384]{1,0:T(8,128)(2,1)S(1)}, u32[]{:S(2)}, u32[]{:S(2)}) collective-permute-start(bf16[8,384]{1,0:T(8,128)(2,1)S(1)} %get-tuple-element.28), channel_id=1, source_target_pairs={{0,1},{1,0},{2,3},{3,2},{4,5},{5,4},{6,7},{7,6},{8,9},{9,8},{10,11... | collective-permute-start | bytes 18440 | tf_op jit(solution)/shard_map/ppermute | solution.py:32
  103.6 5.6 %collective-permute-start.28 = (bf16[8,384]{1,0:T(8,128)(2,1)S(1)}, bf16[8,384]{1,0:T(8,128)(2,1)S(1)}, u32[]{:S(2)}, u32[]{:S(2)}) collective-permute-start(bf16[8,384]{1,0:T(8,128)(2,1)S(1)} %get-tuple-element.28), channel_id=1, source_target_pairs={{0,65},{1,64},{2,67},{3,66},{4,69},{5,68},{6,71},{7,70},{8,73},{9,... | collective-permute-start | bytes 18440 | tf_op jit(solution)/shard_map/ppermute | solution.py:32
  105.1 4.1 %collective-permute-start.27 = (bf16[8,384]{1,0:T(8,128)(2,1)S(1)}, bf16[8,384]{1,0:T(8,128)(2,1)S(1)}, u32[]{:S(2)}, u32[]{:S(2)}) collective-permute-start(bf16[8,384]{1,0:T(8,128)(2,1)S(1)} %get-tuple-element.27.keep0), channel_id=1, source_target_pairs={{0,64},{1,65},{2,66},{3,67},{4,68},{5,69},{6,70},{7,71},{8,72},{9,... | collective-permute-start | bytes 18440 | tf_op jit(solution)/shard_map/ppermute | solution.py:32
  109.8 4.8 %collective-permute-start.29 = (bf16[32,384]{1,0:T(8,128)(2,1)S(1)}, bf16[32,384]{1,0:T(8,128)(2,1)S(1)}, u32[]{:S(2)}, u32[]{:S(2)}) collective-permute-start(bf16[32,384]{1,0:T(8,128)(2,1)S(1)} %heads.1.a0), channel_id=1, source_target_pairs={{0,16},{1,17},{2,18},{3,19},{4,20},{5,21},{6,22},{7,23},{8,24},{9,... | collective-permute-start | bytes 73736 | tf_op jit(solution)/shard_map/ppermute | solution.py:32
  109.9 5.4 %collective-permute-start.30 = (bf16[32,384]{1,0:T(8,128)(2,1)S(1)}, bf16[32,384]{1,0:T(8,128)(2,1)S(1)}, u32[]{:S(2)}, u32[]{:S(2)}) collective-permute-start(bf16[32,384]{1,0:T(8,128)(2,1)S(1)} %heads.1.a0), channel_id=1, source_target_pairs={{0,32},{1,33},{2,34},{3,35},{4,36},{5,37},{6,38},{7,39},{8,40},{9,... | collective-permute-start | bytes 73736 | tf_op jit(solution)/shard_map/ppermute | solution.py:32
  111.6 5.0 %collective-permute-start.31 = (bf16[32,384]{1,0:T(8,128)(2,1)S(1)}, bf16[32,384]{1,0:T(8,128)(2,1)S(1)}, u32[]{:S(2)}, u32[]{:S(2)}) collective-permute-start(bf16[32,384]{1,0:T(8,128)(2,1)S(1)} %heads.1.a0), channel_id=1, source_target_pairs={{0,48},{1,49},{2,50},{3,51},{4,52},{5,53},{6,54},{7,55},{8,56},{9,... | collective-permute-start | bytes 73736 | tf_op jit(solution)/shard_map/ppermute | solution.py:32
  119.5 3.1 %collective-permute-start.32 = (bf16[4,4,2,32,384]{4,3,2,1,0:T(8,128)(2,1)S(1)}, bf16[4,4,2,32,384]{4,3,2,1,0:T(8,128)(2,1)S(1)}, u32[]{:S(2)}, u32[]{:S(2)}) collective-permute-start(bf16[4,4,2,32,384]{4,3,2,1,0:T(8,128)(2,1)S(1)} %share.3), channel_id=1, source_target_pairs={{0,1},{1,0},{2,3},{3,2},{4,5},{5,4},{6,7},{7,6},{8,9},{9,8},{10,11... | collective-permute-start | bytes 2359304 | tf_op jit(solution)/shard_map/ppermute | solution.py:32
  122.8 7.8 %collective-permute-start.33 = (bf16[4,2,32,384]{3,2,1,0:T(8,128)(2,1)S(1)}, bf16[4,2,32,384]{3,2,1,0:T(8,128)(2,1)S(1)}, u32[]{:S(2)}, u32[]{:S(2)}) collective-permute-start(bf16[4,2,32,384]{3,2,1,0:T(8,128)(2,1)S(1)} %get-tuple-element.32), channel_id=1, source_target_pairs={{0,4},{1,5},{2,6},{3,7},{4,0},{5,1},{6,2},{7,3},{8,12},{9,13},{10,... | collective-permute-start | bytes 589832 | tf_op jit(solution)/shard_map/ppermute | solution.py:32
  122.9 12.2 %collective-permute-start.34 = (bf16[4,2,32,384]{3,2,1,0:T(8,128)(2,1)S(1)}, bf16[4,2,32,384]{3,2,1,0:T(8,128)(2,1)S(1)}, u32[]{:S(2)}, u32[]{:S(2)}) collective-permute-start(bf16[4,2,32,384]{3,2,1,0:T(8,128)(2,1)S(1)} %get-tuple-element.31), channel_id=1, source_target_pairs={{0,8},{1,9},{2,10},{3,11},{4,12},{5,13},{6,14},{7,15},{8,0},{9,1},... | collective-permute-start | bytes 589832 | tf_op jit(solution)/shard_map/ppermute | solution.py:32
  125.5 12.2 %collective-permute-start.35 = (bf16[4,2,32,384]{3,2,1,0:T(8,128)(2,1)S(1)}, bf16[4,2,32,384]{3,2,1,0:T(8,128)(2,1)S(1)}, u32[]{:S(2)}, u32[]{:S(2)}) collective-permute-start(bf16[4,2,32,384]{3,2,1,0:T(8,128)(2,1)S(1)} %get-tuple-element.30), channel_id=1, source_target_pairs={{0,12},{1,13},{2,14},{3,15},{4,8},{5,9},{6,10},{7,11},{8,4},{9,5},... | collective-permute-start | bytes 589832 | tf_op jit(solution)/shard_map/ppermute | solution.py:32
  137.8 4.8 %collective-permute-start.36 = (bf16[2,32,384]{2,1,0:T(8,128)(2,1)S(1)}, bf16[2,32,384]{2,1,0:T(8,128)(2,1)S(1)}, u32[]{:S(2)}, u32[]{:S(2)}) collective-permute-start(bf16[2,32,384]{2,1,0:T(8,128)(2,1)S(1)} %get-tuple-element.36), channel_id=1, source_target_pairs={{0,16},{1,17},{2,18},{3,19},{4,20},{5,21},{6,22},{7,23},{8,24},{9,... | collective-permute-start | bytes 147464 | tf_op jit(solution)/shard_map/ppermute | solution.py:32
  138.4 6.5 %collective-permute-start.37 = (bf16[2,32,384]{2,1,0:T(8,128)(2,1)S(1)}, bf16[2,32,384]{2,1,0:T(8,128)(2,1)S(1)}, u32[]{:S(2)}, u32[]{:S(2)}) collective-permute-start(bf16[2,32,384]{2,1,0:T(8,128)(2,1)S(1)} %get-tuple-element.38), channel_id=1, source_target_pairs={{0,32},{1,33},{2,34},{3,35},{4,36},{5,37},{6,38},{7,39},{8,40},{9,... | collective-permute-start | bytes 147464 | tf_op jit(solution)/shard_map/ppermute | solution.py:32
  142.3 5.3 %collective-permute-start.38 = (bf16[2,32,384]{2,1,0:T(8,128)(2,1)S(1)}, bf16[2,32,384]{2,1,0:T(8,128)(2,1)S(1)}, u32[]{:S(2)}, u32[]{:S(2)}) collective-permute-start(bf16[2,32,384]{2,1,0:T(8,128)(2,1)S(1)} %get-tuple-element.37), channel_id=1, source_target_pairs={{0,48},{1,49},{2,50},{3,51},{4,52},{5,53},{6,54},{7,55},{8,56},{9,... | collective-permute-start | bytes 147464 | tf_op jit(solution)/shard_map/ppermute | solution.py:32
  147.6 4.8 %collective-permute-start.39 = (bf16[16,384]{1,0:T(8,128)(2,1)S(1)}, bf16[16,384]{1,0:T(8,128)(2,1)S(1)}, u32[]{:S(2)}, u32[]{:S(2)}) collective-permute-start(bf16[16,384]{1,0:T(8,128)(2,1)S(1)} %get-tuple-element.44), channel_id=1, source_target_pairs={{0,64},{1,65},{2,66},{3,67},{4,68},{5,69},{6,70},{7,71},{8,72},{9,... | collective-permute-start | bytes 36872 | tf_op jit(solution)/shard_map/ppermute | solution.py:32
  149.2 5.2 %collective-permute-start.40 = (bf16[16,384]{1,0:T(8,128)(2,1)S(1)}, bf16[16,384]{1,0:T(8,128)(2,1)S(1)}, u32[]{:S(2)}, u32[]{:S(2)}) collective-permute-start(bf16[16,384]{1,0:T(8,128)(2,1)S(1)} %get-tuple-element.43), channel_id=1, source_target_pairs={{0,2},{1,3},{2,0},{3,1},{4,6},{5,7},{6,4},{7,5},{8,10},{9,11},{10,... | collective-permute-start | bytes 36872 | tf_op jit(solution)/shard_map/ppermute | solution.py:32
  149.7 4.9 %collective-permute-start.41 = (bf16[16,384]{1,0:T(8,128)(2,1)S(1)}, bf16[16,384]{1,0:T(8,128)(2,1)S(1)}, u32[]{:S(2)}, u32[]{:S(2)}) collective-permute-start(bf16[16,384]{1,0:T(8,128)(2,1)S(1)} %get-tuple-element.42), channel_id=1, source_target_pairs={{0,66},{1,67},{2,64},{3,65},{4,70},{5,71},{6,68},{7,69},{8,74},{9,... | collective-permute-start | bytes 36872 | tf_op jit(solution)/shard_map/ppermute | solution.py:32

commit v2 on v1

--- a/solution.py
+++ b/solution.py
@@ -2,6 +2,7 @@
 
 import jax
 import jax.numpy as jnp
+import numpy as np
 from jax import lax
 from jax.experimental import pallas as pl
 from jax.experimental.pallas import tpu as pltpu
@@ -85,7 +86,7 @@
     pick = (iota((128, 32), 1) == row).astype(jnp.bfloat16)
     ids = ids_ref[...]
     high, low = ids >> 8, ids & 255
-    wide = f32dot(pick, high.astype(jnp.float32).astype(jnp.bfloat16)) * 256.0 + f32dot(
+    wide = dot_t(pick, high.astype(jnp.float32).astype(jnp.bfloat16)) * 256.0 + dot_t(
         pick, low.astype(jnp.float32).astype(jnp.bfloat16)
     )
     step = iota((128, 4), 0) & 3
@@ -103,7 +104,7 @@
         functools.partial(embed_kernel, other),
         "embed_part",
         shape16(4, 128, KC),
-        (pos, ids, embed, after),
+        (pos, ids.T, embed, after),
         {0: SMEM, 2: ANY, 3: ANY},
         [pltpu.VMEM((4, vocab, KC), jnp.bfloat16), pltpu.SemaphoreType.DMA((4,))],
         mib=56 if other else 16,
@@ -125,7 +126,7 @@
 
 def settle(parts, after):
     return call(
-        settle_kernel, "settle", shape16(*parts[0].shape), (*parts, after), {4: ANY}, moved=10**5
+        settle_kernel, "settle", shape16(*parts[0].shape), (*parts, after), {4: ANY}, mib=4, moved=10**5
     )
 
 
@@ -145,6 +146,7 @@
         shape16(n * rows, columns),
         (*parts, *after),
         {n + i: ANY for i in range(len(after))},
+        mib=4,
         moved=10**5,
     )
 
@@ -193,7 +195,9 @@
             copies[-1].start()
     chosen_a, label_a = slots_of(ids_a[...], split_qkv, 0)
     chosen_b, label_b = slots_of(ids_b[...], split_out, QKV_CAP)
-    out_ref[:, BLOCK:] = (dot_t(chosen_a, label_a) + dot_t(chosen_b, label_b)).astype(jnp.bfloat16)
+    chosen = jnp.concatenate([chosen_a, chosen_b], axis=1)
+    label = jnp.concatenate([label_a, label_b], axis=1)
+    out_ref[:, BLOCK:] = dot_t(chosen, label).astype(jnp.bfloat16)
 
     def payload(new, pushed, resid, cols):
         value = new[:, cols] - pushed[:, cols].astype(jnp.float32) + resid[:, cols]
@@ -203,8 +207,8 @@
         cols = slice(q * 512, (q + 1) * 512)
         for k in range(6):
             copies[q * 6 + k].wait()
-        packed = f32dot(chosen_a, payload(*bufs[:3], cols))
-        packed = packed + f32dot(chosen_b, payload(*bufs[3:], cols))
+        both = [payload(*bufs[:3], cols), payload(*bufs[3:], cols)]
+        packed = f32dot(chosen, jnp.concatenate(both, axis=0))
         out_ref[:, cols] = packed.astype(jnp.bfloat16)
 
 
@@ -228,6 +232,19 @@
     lane = iota((8, 128), 1)
     scale = jnp.where(lane == 0, 64.0, jnp.where(lane == 1, 1.0, 0.0)).astype(jnp.bfloat16)
     return dot_t(scale, labels)[0:1, :].astype(jnp.int32) - 1
+
+
+def weights_kernel(pos, qkv_ref, out_ref, after, qkv_rows, out_rows, sem):
+    first = pltpu.make_async_copy(
+        qkv_ref.at[pl.ds(pl.multiple_of(pos[0] * 768, 768), 768), :], qkv_rows, sem.at[0]
+    )
+    second = pltpu.make_async_copy(
+        out_ref.at[pl.ds(pl.multiple_of(pos[0] * 48, 48), 48), :], out_rows, sem.at[1]
+    )
+    first.start()
+    second.start()
+    first.wait()
+    second.wait()
 
 
 def place_qkv_kernel(other, pos, arrived_ref, weight_ref, out_ref):
@@ -404,27 +421,21 @@
 def fold(parts):
     rows, columns = parts[0].shape
     return call(
-        fold_kernel, "fold", [shape16(rows // 4, columns)] * 4, tuple(parts), moved=10**5
-    )
-
-
-def rope_tables(lengths, member):
-    half = HD // 2
-    inverse_freq = jnp.power(THETA, -(jnp.arange(half, dtype=jnp.float32) * 2.0 / HD))
-    row_lengths = lax.dynamic_slice_in_dim(lengths, member * 2, 2, 0)
-    positions = (row_lengths[:, None] + jnp.arange(STEPS, dtype=jnp.int32)[None, :]).reshape(-1)
-    angles = positions.astype(jnp.float32)[:, None] * inverse_freq
-    cos, sin = jnp.cos(angles), jnp.sin(angles)
-    return jnp.concatenate([cos, cos], axis=1), jnp.concatenate([-sin, sin], axis=1)
-
-
-def attend_kernel(pos, lengths, own0, own1, other0, other1, cos_ref, sin_ref, cache, o0, o1):
+        fold_kernel, "fold", [shape16(rows // 4, columns)] * 4, tuple(parts), mib=4, moved=10**5
+    )
+
+
+def attend_kernel(pos, lengths, own0, own1, other0, other1, freq_ref, cache, o0, o1):
     member = pos[4]
     own = own0[...].astype(jnp.float32) + own1[...].astype(jnp.float32)
     other = other0[...].astype(jnp.float32) + other1[...].astype(jnp.float32)
     own = own.astype(jnp.bfloat16).astype(jnp.float32)
     other = other.astype(jnp.bfloat16).astype(jnp.float32)
-    cos, sin = cos_ref[...], sin_ref[...]
+    token8 = iota((8, HD), 0)
+    start = jnp.where(token8 >= 4, lengths[member * 2 + 1], lengths[member * 2])
+    angle = (start + (token8 & 3)).astype(jnp.float32) * freq_ref[...]
+    cos, sin = jnp.cos(angle), jnp.sin(angle)
+    sin = jnp.where(iota((8, HD), 1) < HD // 2, -sin, sin)
 
     def rotate(u):
         return (u * cos + pltpu.roll(u, HD // 2, 1) * sin).astype(jnp.bfloat16)
@@ -470,12 +481,14 @@
         out_ref[...] = jnp.concatenate(blocks, axis=1).astype(jnp.bfloat16)
 
 
-def attend(pos, lengths, own, other, tables, kv_cache):
+def attend(pos, lengths, own, other, kv_cache):
+    freq = np.power(THETA, -(np.arange(HD // 2, dtype=np.float64) * 2.0 / HD)).astype(np.float32)
+    freq = jnp.asarray(np.tile(freq, 2)[None, :])
     return call(
         attend_kernel,
         "attend",
         [shape16(8, 384)] * 2,
-        (pos, lengths, *own, *other, *tables, kv_cache),
+        (pos, lengths, *own, *other, freq, kv_cache),
         {0: SMEM, 1: SMEM},
         mib=20,
         flops=8 * 48 * CACHE * HD,
@@ -526,17 +539,24 @@
         qkv_map, out_map, new_qkv, pushed_qkv, resid_qkv, new_out, pushed_out, resid_out
     )
     arrived = lax.all_to_all(packed, "tensor", split_axis=0, concat_axis=0, tiled=True)
-    qkv_rows = lax.dynamic_slice_in_dim(qkv_weight, r * 768, 768, 0)
-    out_rows = lax.dynamic_slice_in_dim(out_weight, r * 48, 48, 0)
-    first_matrix = place_qkv(pos, arrived, qkv_rows, 0)
-    last_matrix = place_qkv(pos, arrived, qkv_rows, 1)
-    out_part = place_out(pos, arrived, out_rows)
-
     give = embed_half(pos, token_ids, embed, packed, 1)
     got = swap(give, 1 << CORE)
     keep = embed_half(pos, token_ids, embed, give, 0)
     y_parts = [keep[s] + got[s] for s in range(4)]
     y_got = [swap(y_parts[s], s << Y) for s in range(1, 4)]
+    qkv_rows, out_rows = call(
+        weights_kernel,
+        "weights",
+        [shape16(768, 512), shape16(48, D)],
+        (pos, qkv_weight, out_weight, y_parts[3]),
+        {0: SMEM, 1: ANY, 2: ANY, 3: ANY},
+        [pltpu.SemaphoreType.DMA((2,))],
+        mib=4,
+        moved=3 * 1024 * 1024,
+    )
+    first_matrix = place_qkv(pos, arrived, qkv_rows, 0)
+    last_matrix = place_qkv(pos, arrived, qkv_rows, 1)
+    out_part = place_out(pos, arrived, out_rows)
     z_all = y_parts[0] + y_got[0] + y_got[1] + y_got[2]
     z_got = [swap(z_all[s * 32 : (s + 1) * 32], s << Z) for s in range(1, 4)]
     x_all = z_all[:32] + z_got[0] + z_got[1] + z_got[2]
@@ -553,8 +573,7 @@
     own = (blocks[0], swap(blocks[2], x_bit))
     other = (swap(blocks[1], core_bit), swap(blocks[3], core_bit | x_bit))
 
-    tables = rope_tables(lengths, core)
-    head_keep, head_give = attend(pos, lengths, own, other, tables, kv_cache)
+    head_keep, head_give = attend(pos, lengths, own, other, kv_cache)
     head_pair = call(
         heads_kernel,
         "heads",
@@ -568,6 +587,7 @@
             out_part,
         ),
         {0: SMEM, 5: ANY},
+        mib=4,
         moved=10**5,
     )
     heads = [head_pair] + [swap(head_pair, s << Y) for s in range(1, 4)]
@@ -589,6 +609,7 @@
         "finish",
         shape16(lengths.shape[0], STEPS, OC),
         (x_parts[0, :16], *x_got),
+        mib=4,
         moved=10**5,
     )
 

time: 156 us -> 144 us (0.923)
  starting transfers between devices: 61.3 us -> 57.1 us
  local copies, waits for them, and re-layouts: 10.2 us -> 7.77 us
  other arithmetic: 2.63 us -> 0.49 us
    ppermute x42, starting transfers between devices: 53.3 us -> 49.1 us  [swap(): return lax.ppermute(value, AXES, [(i, i ^ mask) for i in range(128)])]
    dynamic_slice x3 -> x0, local copies, waits for them, and re-layouts: 3.18 us -> none  [the longest x1 1.92 us: body(): out_rows = lax.dynamic_slice_in_dim(out_weight, r * 48, 48, 0)]
    pallas_call x16 -> x17, Pallas kernels: 35 us -> 33.7 us  [call(): pl.pallas_call(kernel, out_shape=out_shape, in_specs=[specs.get(i, vmem)...]
    unnamed x33 -> x22, local copies, waits for them, and re-layouts: 6.28 us -> 7.12 us
  transfers between devices with their start and end apart: 43 -> 43, of which waited for: 20 -> 19; matrix products, arithmetic and copies ran while one was open for 4% -> 1% of each run, Pallas kernels for 13% -> 14%
where the time goes in v2:
time: 144 us
  starting transfers between devices  57.1 us (40%)
  waiting for transfers between devices  44.1 us (31%)
  Pallas kernels  33.7 us (23%)
  local copies, waits for them, and re-layouts  7.77 us (5%)
    ppermute x42, starting transfers between devices, swap(): return lax.ppermute(value, AXES, [(i, i ^ mask) for i in range(128)])  49.1 us
    ppermute x42, waiting for transfers between devices, swap(): return lax.ppermute(value, AXES, [(i, i ^ mask) for i in range(128)])  44.1 us
    pallas_call x17, Pallas kernels, call(): pl.pallas_call(kernel, out_shape=out_shape, in_specs=[specs.get(i, vmem)...  33.7 us
    all_to_all x1, starting transfers between devices, body(): lax.all_to_all(packed, 'tensor', split_axis=0, concat_axis=0, tiled=True)  7.97 us
    unnamed x22, local copies, waits for them, and re-layouts  7.12 us
  transfers between devices with their start and end apart: 43, of which 19 were waited for; matrix products, arithmetic and copies ran while one was open for 1% of the time, Pallas kernels for 14%

profile of v2, /device:TPU:0, one launch (start us, length us, event | category | flops | bytes accessed | tf_op | source)
XLA Modules:
  0.0 143.7 jit_solution(10545562166078103301)
XLA Ops:
  0.0 5.8 %pack_blocks.1.after = bf16[512,2176]{1,0:T(8,128)(2,1)} custom-call(s32[1,192]{1,0:T(1,128)} %bitcast.77, s32[1,144]{1,0:T(1,128)} %bitcast.78, f32[192,2048]{1,0:T(8,128)} %refs_0_.1, bf16[192,2048]{1,0:T(8,128)(2,1)} %refs_1_.1, f32[192,2048]{1,0:T(8,128)} %refs_2_.1, f32[144,2048]{1,0:T(8,128)} %refs_3_.1, bf16[144,2048]{1,0:T(8,128)(2,1)} %refs_4_.1, ...), custom_call_target="tpu_custom_call" | custom-call | flops 704643072 | bytes 6881280 | tf_op jit(solution)/shard_map/pack_blocks/pallas_call | solution.py:51
  5.8 8.0 %all-to-all-start = ((bf16[16,32,2176]{2,1,0:T(8,128)(2,1)}), bf16[16,32,2176]{2,1,0:T(8,128)(2,1)S(1)}, u32[]{:S(2)}, u32[]{:S(2)}) async-start(bf16[16,32,2176]{2,1,0:T(8,128)(2,1)} %bitcast.76), calls=%async_computation | async-start | bytes 4456448 | tf_op jit(solution)/shard_map/all_to_all | solution.py:541
  13.9 0.6 stack.32.pos
  14.5 3.8 %embed_part.2.after = bf16[4,128,768]{2,1,0:T(8,128)(2,1)} custom-call(s32[7]{0:T(128)} %stack.32.pos, s32[4,32]{1,0:T(4,128)} %bitcast.74, bf16[256,6144]{1,0:T(8,128)(2,1)} %embed_ref.3, bf16[512,2176]{1,0:T(8,128)(2,1)} %pack_blocks.1.after), custom_call_target="tpu_custom_call" | custom-call | flops 201326592 | bytes 1572864 | tf_op jit(solution)/shard_map/embed_part/pallas_call | solution.py:51
  18.8 1.1 copy-done.4
  19.9 1.9 %embed_part.3 = bf16[4,128,768]{2,1,0:T(8,128)(2,1)S(1)} custom-call(s32[7]{0:T(128)S(1)} %copy-done.5, s32[4,32]{1,0:T(4,128)S(1)} %bitcast.75, bf16[256,6144]{1,0:T(8,128)(2,1)S(1)} %copy-done, bf16[4,128,768]{2,1,0:T(8,128)(2,1)S(1)} %copy-done.4), custom_call_target="tpu_custom_call" | custom-call | flops 201326592 | bytes 1572864 | tf_op jit(solution)/shard_map/embed_part/pallas_call | solution.py:51
  21.9 1.7 %collective-permute-start.1 = (bf16[128,768]{1,0:T(8,128)(2,1)S(1)}, bf16[128,768]{1,0:T(8,128)(2,1)S(1)}, u32[]{:S(2)}, u32[]{:S(2)}) collective-permute-start(bf16[128,768]{1,0:T(8,128)(2,1)S(1)} %get-tuple-element.37), channel_id=1, source_target_pairs={{0,16},{1,17},{2,18},{3,19},{4,20},{5,21},{6,22},{7,23},{8,24},{9,... | collective-permute-start | bytes 589832 | tf_op jit(solution)/shard_map/ppermute | solution.py:33
  23.6 2.9 %collective-permute-start.2 = (bf16[128,768]{1,0:T(8,128)(2,1)S(1)}, bf16[128,768]{1,0:T(8,128)(2,1)S(1)}, u32[]{:S(2)}, u32[]{:S(2)}) collective-permute-start(bf16[128,768]{1,0:T(8,128)(2,1)S(1)} %get-tuple-element.39), channel_id=1, source_target_pairs={{0,32},{1,33},{2,34},{3,35},{4,36},{5,37},{6,38},{7,39},{8,40},{9,... | collective-permute-start | bytes 589832 | tf_op jit(solution)/shard_map/ppermute | solution.py:33
  26.7 3.1 %collective-permute-done.1 = bf16[128,768]{1,0:T(8,128)(2,1)S(1)} collective-permute-done((bf16[128,768]{1,0:T(8,128)(2,1)S(1)}, bf16[128,768]{1,0:T(8,128)(2,1)S(1)}, u32[]{:S(2)}, u32[]{:S(2)}) %collective-permute-start.1) | collective-permute-done | bytes 196640 | tf_op jit(solution)/shard_map/ppermute | solution.py:33
  29.8 5.9 %collective-permute-done.2 = bf16[128,768]{1,0:T(8,128)(2,1)S(1)} collective-permute-done((bf16[128,768]{1,0:T(8,128)(2,1)S(1)}, bf16[128,768]{1,0:T(8,128)(2,1)S(1)}, u32[]{:S(2)}, u32[]{:S(2)}) %collective-permute-start.2) | collective-permute-done | bytes 196640 | tf_op jit(solution)/shard_map/ppermute | solution.py:33
  35.7 2.6 %collective-permute-done.3 = bf16[128,768]{1,0:T(8,128)(2,1)S(1)} collective-permute-done((bf16[128,768]{1,0:T(8,128)(2,1)S(1)}, bf16[128,768]{1,0:T(8,128)(2,1)S(1)}, u32[]{:S(2)}, u32[]{:S(2)}) %collective-permute-start.3) | collective-permute-done | bytes 196640 | tf_op jit(solution)/shard_map/ppermute | solution.py:33
  38.3 2.0 %collective-permute-start.4 = (bf16[32,768]{1,0:T(8,128)(2,1)S(1)}, bf16[32,768]{1,0:T(8,128)(2,1)S(1)}, u32[]{:S(2)}, u32[]{:S(2)}) collective-permute-start(bf16[32,768]{1,0:T(8,128)(2,1)S(1)} %get-tuple-element.43), channel_id=1, source_target_pairs={{0,4},{1,5},{2,6},{3,7},{4,0},{5,1},{6,2},{7,3},{8,12},{9,13},{10,... | collective-permute-start | bytes 147464 | tf_op jit(solution)/shard_map/ppermute | solution.py:33
  40.3 2.1 %collective-permute-start.6 = (bf16[32,768]{1,0:T(8,128)(2,1)S(1)}, bf16[32,768]{1,0:T(8,128)(2,1)S(1)}, u32[]{:S(2)}, u32[]{:S(2)}) collective-permute-start(bf16[32,768]{1,0:T(8,128)(2,1)S(1)} %get-tuple-element.44), channel_id=1, source_target_pairs={{0,12},{1,13},{2,14},{3,15},{4,8},{5,9},{6,10},{7,11},{8,4},{9,5},... | collective-permute-start | bytes 147464 | tf_op jit(solution)/shard_map/ppermute | solution.py:33
  42.4 0.6 collective-permute-start.5
  43.0 2.8 %copy-done.1 = bf16[6144,512]{1,0:T(8,128)(2,1)S(1)} copy-done((bf16[6144,512]{1,0:T(8,128)(2,1)S(1)}, bf16[6144,512]{1,0:T(8,128)(2,1)}, u32[]{:S(2)}) %copy-start.1) | copy-done | bytes 6291480
  45.8 2.3 %copy-done.2 = bf16[384,6144]{1,0:T(8,128)(2,1)S(1)} copy-done((bf16[384,6144]{1,0:T(8,128)(2,1)S(1)}, bf16[384,6144]{1,0:T(8,128)(2,1)}, u32[]{:S(2)}) %copy-start.2) | copy-done | bytes 4718616
  48.1 0.7 weights.1
  48.9 0.8 copy-done.9
  49.8 2.8 %collective-permute-start.9 = (bf16[32,768]{1,0:T(8,128)(2,1)S(1)}, bf16[32,768]{1,0:T(8,128)(2,1)S(1)}, u32[]{:S(2)}, u32[]{:S(2)}) collective-permute-start(bf16[32,768]{1,0:T(8,128)(2,1)S(1)} %fusion.30.a), channel_id=1, source_target_pairs={{0,66},{1,67},{2,64},{3,65},{4,70},{5,71},{6,68},{7,69},{8,74},{9,... | collective-permute-start | bytes 147464 | tf_op jit(solution)/shard_map/ppermute | solution.py:33
  52.9 1.0 collective-permute-start.7
  53.9 2.9 %place_qkv.2.after.matrix_ref = bf16[3072,512]{1,0:T(8,128)(2,1)S(1)} custom-call(s32[7]{0:T(128)S(1)} %copy-done.5, bf16[512,2176]{1,0:T(8,128)(2,1)S(1)} %bitcast.71, bf16[768,512]{1,0:T(8,128)(2,1)S(1)} %get-tuple-element.19.weight_ref), custom_call_target="tpu_custom_call" | custom-call | flops 1610612736 | bytes 6291456 | tf_op jit(solution)/shard_map/place_qkv/pallas_call | solution.py:51
  56.8 1.3 collective-permute-done.8.c
  58.3 2.7 %collective-permute-start.12 = (bf16[32,768]{1,0:T(8,128)(2,1)S(1)}, bf16[32,768]{1,0:T(8,128)(2,1)S(1)}, u32[]{:S(2)}, u32[]{:S(2)}) collective-permute-start(bf16[32,768]{1,0:T(8,128)(2,1)S(1)} %settle.1.refs_0_), channel_id=1, source_target_pairs={{0,12},{1,13},{2,14},{3,15},{4,8},{5,9},{6,10},{7,11},{8,4},{9,5},... | collective-permute-start | bytes 147464 | tf_op jit(solution)/shard_map/ppermute | solution.py:33
  61.0 0.9 collective-permute-start.11
  61.9 0.6 collective-permute-start.10
  62.5 2.5 %place_qkv.3.refs_4_.matrix_ref = bf16[3072,512]{1,0:T(8,128)(2,1)S(1)} custom-call(s32[7]{0:T(128)S(1)} %copy-done.5, bf16[512,2176]{1,0:T(8,128)(2,1)S(1)} %bitcast.72, bf16[768,512]{1,0:T(8,128)(2,1)S(1)} %get-tuple-element.19.weight_ref), custom_call_target="tpu_custom_call" | custom-call | flops 1610612736 | bytes 6291456 | tf_op jit(solution)/shard_map/place_qkv/pallas_call | solution.py:51
  65.0 1.7 %collective-permute-done.11.refs_2_ = bf16[32,768]{1,0:T(8,128)(2,1)S(1)} collective-permute-done((bf16[32,768]{1,0:T(8,128)(2,1)S(1)}, bf16[32,768]{1,0:T(8,128)(2,1)S(1)}, u32[]{:S(2)}, u32[]{:S(2)}) %collective-permute-start.11) | collective-permute-done | bytes 49184 | tf_op jit(solution)/shard_map/ppermute | solution.py:33
  67.0 0.7 collective-permute-start.16
  67.7 3.1 %collective-permute-start.14 = (bf16[128,768]{1,0:T(8,128)(2,1)S(1)}, bf16[128,768]{1,0:T(8,128)(2,1)S(1)}, u32[]{:S(2)}, u32[]{:S(2)}) collective-permute-start(bf16[128,768]{1,0:T(8,128)(2,1)S(1)} %stack.33.p0), channel_id=1, source_target_pairs={{0,16},{1,17},{2,18},{3,19},{4,20},{5,21},{6,22},{7,23},{8,24},{9,... | collective-permute-start | bytes 589832 | tf_op jit(solution)/shard_map/ppermute | solution.py:33
  70.8 4.9 %collective-permute-done.18.p3 = bf16[128,768]{1,0:T(8,128)(2,1)S(1)} collective-permute-done((bf16[128,768]{1,0:T(8,128)(2,1)S(1)}, bf16[128,768]{1,0:T(8,128)(2,1)S(1)}, u32[]{:S(2)}, u32[]{:S(2)}) %collective-permute-start.18) | collective-permute-done | bytes 196640 | tf_op jit(solution)/shard_map/ppermute | solution.py:33
  76.6 1.8 %project_first.1 = (f32[128,512]{1,0:T(8,128)S(1)}, f32[128,128]{1,0:T(8,128)S(1)}) custom-call(s32[7]{0:T(128)S(1)} %copy-done.5, bf16[128,768]{1,0:T(8,128)(2,1)S(1)} %stack.33.p0, bf16[128,768]{1,0:T(8,128)(2,1)S(1)} %collective-permute-done.14.p1, bf16[128,768]{1,0:T(8,128)(2,1)S(1)} %collective-permute-done.16.p2, ...), custom_call_target="tpu_custom_call" | custom-call | flops 402653184 | bytes 4194304 | tf_op jit(solution)/shard_map/project_first/pallas_call | solution.py:51
  78.5 1.8 %project_last.1 = (bf16[32,512]{1,0:T(8,128)(2,1)S(1)}, bf16[32,512]{1,0:T(8,128)(2,1)S(1)}, bf16[32,512]{1,0:T(8,128)(2,1)S(1)}, bf16[32,512]{1,0:T(8,128)(2,1)S(1)}) custom-call(s32[7]{0:T(128)S(1)} %copy-done.5, bf16[128,768]{1,0:T(8,128)(2,1)S(1)} %collective-permute-done.13.p0, bf16[128,768]{1,0:T(8,128)(2,1)S(1)} %collective-permute-done.15.p1, ...), custom_call_target="tpu_custom_call" | custom-call | flops 402653184 | bytes 4194304 | tf_op jit(solution)/shard_map/project_last/pallas_call | solution.py:51
  80.4 2.5 %collective-permute-start.21 = (bf16[32,512]{1,0:T(8,128)(2,1)S(1)}, bf16[32,512]{1,0:T(8,128)(2,1)S(1)}, u32[]{:S(2)}, u32[]{:S(2)}) collective-permute-start(bf16[32,512]{1,0:T(8,128)(2,1)S(1)} %get-tuple-element.24), channel_id=1, source_target_pairs={{0,32},{1,33},{2,34},{3,35},{4,36},{5,37},{6,38},{7,39},{8,40},{9,... | collective-permute-start | bytes 98312 | tf_op jit(solution)/shard_map/ppermute | solution.py:33
  82.9 2.2 %collective-permute-start.22 = (bf16[32,512]{1,0:T(8,128)(2,1)S(1)}, bf16[32,512]{1,0:T(8,128)(2,1)S(1)}, u32[]{:S(2)}, u32[]{:S(2)}) collective-permute-start(bf16[32,512]{1,0:T(8,128)(2,1)S(1)} %get-tuple-element.25), channel_id=1, source_target_pairs={{0,48},{1,49},{2,50},{3,51},{4,52},{5,53},{6,54},{7,55},{8,56},{9,... | collective-permute-start | bytes 98312 | tf_op jit(solution)/shard_map/ppermute | solution.py:33
  85.1 0.8 collective-permute-done.21.c
  85.9 2.1 %collective-permute-done.22.d = bf16[32,512]{1,0:T(8,128)(2,1)S(1)} collective-permute-done((bf16[32,512]{1,0:T(8,128)(2,1)S(1)}, bf16[32,512]{1,0:T(8,128)(2,1)S(1)}, u32[]{:S(2)}, u32[]{:S(2)}) %collective-permute-start.22) | collective-permute-done | bytes 32800 | tf_op jit(solution)/shard_map/ppermute | solution.py:33
  88.4 1.9 %collective-permute-start.25 = (bf16[8,512]{1,0:T(8,128)(2,1)S(1)}, bf16[8,512]{1,0:T(8,128)(2,1)S(1)}, u32[]{:S(2)}, u32[]{:S(2)}) collective-permute-start(bf16[8,512]{1,0:T(8,128)(2,1)S(1)} %get-tuple-element.29), channel_id=1, source_target_pairs={{0,65},{1,64},{2,67},{3,66},{4,69},{5,68},{6,71},{7,70},{8,73},{9,... | collective-permute-start | bytes 24584 | tf_op jit(solution)/shard_map/ppermute | solution.py:33
  90.3 1.5 %collective-permute-done.23.own1 = bf16[8,512]{1,0:T(8,128)(2,1)S(1)} collective-permute-done((bf16[8,512]{1,0:T(8,128)(2,1)S(1)}, bf16[8,512]{1,0:T(8,128)(2,1)S(1)}, u32[]{:S(2)}, u32[]{:S(2)}) %collective-permute-start.23) | collective-permute-done | bytes 8224 | tf_op jit(solution)/shard_map/ppermute | solution.py:33
  91.8 2.0 %attend.1 = (bf16[8,384]{1,0:T(8,128)(2,1)S(1)}, bf16[8,384]{1,0:T(8,128)(2,1)S(1)}) custom-call(s32[7]{0:T(128)S(1)} %copy-done.5, s32[4]{0:T(128)S(1)} %copy-done.7, bf16[8,512]{1,0:T(8,128)(2,1)S(1)} %get-tuple-element.26.own0, bf16[8,512]{1,0:T(8,128)(2,1)S(1)} %collective-permute-done.23.own1, bf16[8,512]{1,0:T(8,128)(2,1)S(1)} %collective-permute-done.24.other0, ...), custom_call_target="tpu_custom_call" | custom-call | flops 201326592 | bytes 5242880 | tf_op jit(solution)/shard_map/attend/pallas_call | solution.py:51
  93.9 1.6 %collective-permute-start.28 = (bf16[8,384]{1,0:T(8,128)(2,1)S(1)}, bf16[8,384]{1,0:T(8,128)(2,1)S(1)}, u32[]{:S(2)}, u32[]{:S(2)}) collective-permute-start(bf16[8,384]{1,0:T(8,128)(2,1)S(1)} %get-tuple-element.31), channel_id=1, source_target_pairs={{0,65},{1,64},{2,67},{3,66},{4,69},{5,68},{6,71},{7,70},{8,73},{9,... | collective-permute-start | bytes 18440 | tf_op jit(solution)/shard_map/ppermute | solution.py:33
  95.5 0.6 collective-permute-start.27
  96.1 3.5 %place_out.1.after.matrix_ref = bf16[384,6144]{1,0:T(8,128)(2,1)S(1)} custom-call(s32[7]{0:T(128)S(1)} %copy-done.5, bf16[512,2176]{1,0:T(8,128)(2,1)S(1)} %bitcast.73, bf16[48,6144]{1,0:T(8,128)(2,1)S(1)} %copy-done.10), custom_call_target="tpu_custom_call" | custom-call | flops 2415919104 | bytes 7340032 | tf_op jit(solution)/shard_map/place_out/pallas_call | solution.py:51
  99.7 0.6 heads.1.a0
  100.2 2.2 %collective-permute-start.31 = (bf16[32,384]{1,0:T(8,128)(2,1)S(1)}, bf16[32,384]{1,0:T(8,128)(2,1)S(1)}, u32[]{:S(2)}, u32[]{:S(2)}) collective-permute-start(bf16[32,384]{1,0:T(8,128)(2,1)S(1)} %heads.1.a0), channel_id=1, source_target_pairs={{0,48},{1,49},{2,50},{3,51},{4,52},{5,53},{6,54},{7,55},{8,56},{9,... | collective-permute-start | bytes 73736 | tf_op jit(solution)/shard_map/ppermute | solution.py:33
  102.5 1.9 %collective-permute-start.29 = (bf16[32,384]{1,0:T(8,128)(2,1)S(1)}, bf16[32,384]{1,0:T(8,128)(2,1)S(1)}, u32[]{:S(2)}, u32[]{:S(2)}) collective-permute-start(bf16[32,384]{1,0:T(8,128)(2,1)S(1)} %heads.1.a0), channel_id=1, source_target_pairs={{0,16},{1,17},{2,18},{3,19},{4,20},{5,21},{6,22},{7,23},{8,24},{9,... | collective-permute-start | bytes 73736 | tf_op jit(solution)/shard_map/ppermute | solution.py:33
  104.4 0.9 collective-permute-done.31.a3
  105.4 2.5 %collective-permute-done.30.a2 = bf16[32,384]{1,0:T(8,128)(2,1)S(1)} collective-permute-done((bf16[32,384]{1,0:T(8,128)(2,1)S(1)}, bf16[32,384]{1,0:T(8,128)(2,1)S(1)}, u32[]{:S(2)}, u32[]{:S(2)}) %collective-permute-start.30) | collective-permute-done | bytes 24608 | tf_op jit(solution)/shard_map/ppermute | solution.py:33
  107.8 2.8 %share.3 = bf16[4,4,2,32,384]{4,3,2,1,0:T(8,128)(2,1)S(1)} custom-call(s32[7]{0:T(128)S(1)} %copy-done.5, bf16[32,384]{1,0:T(8,128)(2,1)S(1)} %heads.1.a0, bf16[32,384]{1,0:T(8,128)(2,1)S(1)} %collective-permute-done.29.a1, bf16[32,384]{1,0:T(8,128)(2,1)S(1)} %collective-permute-done.30.a2, bf16[32,384]{1,0:T(8,128)(2,1)S(1)} %collective-permute-done.31.a3, ...), custom_call_target="tpu_custom_call" | custom-call | flops 301989888 | bytes 4194304 | tf_op jit(solution)/shard_map/share/pallas_call | solution.py:51
  110.9 2.8 %share.2 = bf16[4,4,2,32,384]{4,3,2,1,0:T(8,128)(2,1)S(1)} custom-call(s32[7]{0:T(128)S(1)} %copy-done.5, bf16[32,384]{1,0:T(8,128)(2,1)S(1)} %heads.1.a0, bf16[32,384]{1,0:T(8,128)(2,1)S(1)} %collective-permute-done.29.a1, bf16[32,384]{1,0:T(8,128)(2,1)S(1)} %collective-permute-done.30.a2, bf16[32,384]{1,0:T(8,128)(2,1)S(1)} %collective-permute-done.31.a3, ...), custom_call_target="tpu_custom_call" | custom-call | flops 301989888 | bytes 4194304 | tf_op jit(solution)/shard_map/share/pallas_call | solution.py:51
  114.0 1.5 %collective-permute-start.35 = (bf16[4,2,32,384]{3,2,1,0:T(8,128)(2,1)S(1)}, bf16[4,2,32,384]{3,2,1,0:T(8,128)(2,1)S(1)}, u32[]{:S(2)}, u32[]{:S(2)}) collective-permute-start(bf16[4,2,32,384]{3,2,1,0:T(8,128)(2,1)S(1)} %get-tuple-element.34), channel_id=1, source_target_pairs={{0,12},{1,13},{2,14},{3,15},{4,8},{5,9},{6,10},{7,11},{8,4},{9,5},... | collective-permute-start | bytes 589832 | tf_op jit(solution)/shard_map/ppermute | solution.py:33
  115.5 0.9 collective-permute-start.34
  116.4 1.8 %collective-permute-start.33 = (bf16[4,2,32,384]{3,2,1,0:T(8,128)(2,1)S(1)}, bf16[4,2,32,384]{3,2,1,0:T(8,128)(2,1)S(1)}, u32[]{:S(2)}, u32[]{:S(2)}) collective-permute-start(bf16[4,2,32,384]{3,2,1,0:T(8,128)(2,1)S(1)} %get-tuple-element.36), channel_id=1, source_target_pairs={{0,4},{1,5},{2,6},{3,7},{4,0},{5,1},{6,2},{7,3},{8,12},{9,13},{10,... | collective-permute-start | bytes 589832 | tf_op jit(solution)/shard_map/ppermute | solution.py:33
  118.2 8.6 %collective-permute-done.35 = bf16[4,2,32,384]{3,2,1,0:T(8,128)(2,1)S(1)} collective-permute-done((bf16[4,2,32,384]{3,2,1,0:T(8,128)(2,1)S(1)}, bf16[4,2,32,384]{3,2,1,0:T(8,128)(2,1)S(1)}, u32[]{:S(2)}, u32[]{:S(2)}) %collective-permute-start.35) | collective-permute-done | bytes 196640 | tf_op jit(solution)/shard_map/ppermute | solution.py:33
  126.8 0.6 collective-permute-done.33
  128.0 2.2 %collective-permute-start.38 = (bf16[2,32,384]{2,1,0:T(8,128)(2,1)S(1)}, bf16[2,32,384]{2,1,0:T(8,128)(2,1)S(1)}, u32[]{:S(2)}, u32[]{:S(2)}) collective-permute-start(bf16[2,32,384]{2,1,0:T(8,128)(2,1)S(1)} %get-tuple-element.41), channel_id=1, source_target_pairs={{0,48},{1,49},{2,50},{3,51},{4,52},{5,53},{6,54},{7,55},{8,56},{9,... | collective-permute-start | bytes 147464 | tf_op jit(solution)/shard_map/ppermute | solution.py:33
  130.2 1.5 %collective-permute-start.37 = (bf16[2,32,384]{2,1,0:T(8,128)(2,1)S(1)}, bf16[2,32,384]{2,1,0:T(8,128)(2,1)S(1)}, u32[]{:S(2)}, u32[]{:S(2)}) collective-permute-start(bf16[2,32,384]{2,1,0:T(8,128)(2,1)S(1)} %get-tuple-element.42), channel_id=1, source_target_pairs={{0,32},{1,33},{2,34},{3,35},{4,36},{5,37},{6,38},{7,39},{8,40},{9,... | collective-permute-start | bytes 147464 | tf_op jit(solution)/shard_map/ppermute | solution.py:33
  131.9 1.9 %collective-permute-done.38 = bf16[2,32,384]{2,1,0:T(8,128)(2,1)S(1)} collective-permute-done((bf16[2,32,384]{2,1,0:T(8,128)(2,1)S(1)}, bf16[2,32,384]{2,1,0:T(8,128)(2,1)S(1)}, u32[]{:S(2)}, u32[]{:S(2)}) %collective-permute-start.38) | collective-permute-done | bytes 49184 | tf_op jit(solution)/shard_map/ppermute | solution.py:33
  133.8 1.9 %collective-permute-done.37 = bf16[2,32,384]{2,1,0:T(8,128)(2,1)S(1)} collective-permute-done((bf16[2,32,384]{2,1,0:T(8,128)(2,1)S(1)}, bf16[2,32,384]{2,1,0:T(8,128)(2,1)S(1)}, u32[]{:S(2)}, u32[]{:S(2)}) %collective-permute-start.37) | collective-permute-done | bytes 49184 | tf_op jit(solution)/shard_map/ppermute | solution.py:33
  135.8 2.1 %collective-permute-start.41 = (bf16[16,384]{1,0:T(8,128)(2,1)S(1)}, bf16[16,384]{1,0:T(8,128)(2,1)S(1)}, u32[]{:S(2)}, u32[]{:S(2)}) collective-permute-start(bf16[16,384]{1,0:T(8,128)(2,1)S(1)} %get-tuple-element.46), channel_id=1, source_target_pairs={{0,66},{1,67},{2,64},{3,65},{4,70},{5,71},{6,68},{7,69},{8,74},{9,... | collective-permute-start | bytes 36872 | tf_op jit(solution)/shard_map/ppermute | solution.py:33
  137.9 1.5 %collective-permute-start.40 = (bf16[16,384]{1,0:T(8,128)(2,1)S(1)}, bf16[16,384]{1,0:T(8,128)(2,1)S(1)}, u32[]{:S(2)}, u32[]{:S(2)}) collective-permute-start(bf16[16,384]{1,0:T(8,128)(2,1)S(1)} %get-tuple-element.47), channel_id=1, source_target_pairs={{0,2},{1,3},{2,0},{3,1},{4,6},{5,7},{6,4},{7,5},{8,10},{9,11},{10,... | collective-permute-start | bytes 36872 | tf_op jit(solution)/shard_map/ppermute | solution.py:33
  139.4 0.6 collective-permute-start.39
  140.0 0.8 collective-permute-done.41.d
  140.8 2.3 %collective-permute-done.40.c = bf16[16,384]{1,0:T(8,128)(2,1)S(1)} collective-permute-done((bf16[16,384]{1,0:T(8,128)(2,1)S(1)}, bf16[16,384]{1,0:T(8,128)(2,1)S(1)}, u32[]{:S(2)}, u32[]{:S(2)}) %collective-permute-start.40) | collective-permute-done | bytes 12320 | tf_op jit(solution)/shard_map/ppermute | solution.py:33
  143.1 0.6 finish.1
  (70 shorter events, 4.6 us)
Async XLA Ops:
  5.8 48.1 %all-to-all-start = ((bf16[16,32,2176]{2,1,0:T(8,128)(2,1)}), bf16[16,32,2176]{2,1,0:T(8,128)(2,1)S(1)}, u32[]{:S(2)}, u32[]{:S(2)}) async-start(bf16[16,32,2176]{2,1,0:T(8,128)(2,1)} %bitcast.76), calls=%async_computation | async-start | bytes 4456448 | tf_op jit(solution)/shard_map/all_to_all | solution.py:541
  13.8 5.0 %copy-start.6 = (s32[32,4]{0,1:T(4,128)S(1)}, s32[32,4]{0,1:T(4,128)}, u32[]{:S(2)}) copy-start(s32[32,4]{0,1:T(4,128)} %param.15) | copy-start | bytes 1540
  14.5 4.3 %copy-start = (bf16[256,6144]{1,0:T(8,128)(2,1)S(1)}, bf16[256,6144]{1,0:T(8,128)(2,1)}, u32[]{:S(2)}) copy-start(bf16[256,6144]{1,0:T(8,128)(2,1)} %embed_ref.3) | copy-start | bytes 9437188
  14.5 4.3 %copy-start.5 = (s32[7]{0:T(128)S(1)}, s32[7]{0:T(128)}, u32[]{:S(2)}) copy-start(s32[7]{0:T(128)} %stack.32.pos) | copy-start | bytes 88
  18.3 3.5 %collective-permute-start = (bf16[4,128,768]{2,1,0:T(8,128)(2,1)}, bf16[4,128,768]{2,1,0:T(8,128)(2,1)S(1)}, u32[]{:S(2)}, u32[]{:S(2)}) collective-permute-start(bf16[4,128,768]{2,1,0:T(8,128)(2,1)} %embed_part.2.after), channel_id=1, source_target_pairs={{0,1},{1,0},{2,3},{3,2},{4,5},{5,4},{6,7},{7,6},{8,9},{9,8},{10,11... | collective-permute-start | bytes 2359304 | tf_op jit(solution)/shard_map/ppermute | solution.py:33
  18.8 1.1 copy-start.4
  21.9 7.8 %collective-permute-start.1 = (bf16[128,768]{1,0:T(8,128)(2,1)S(1)}, bf16[128,768]{1,0:T(8,128)(2,1)S(1)}, u32[]{:S(2)}, u32[]{:S(2)}) collective-permute-start(bf16[128,768]{1,0:T(8,128)(2,1)S(1)} %get-tuple-element.37), channel_id=1, source_target_pairs={{0,16},{1,17},{2,18},{3,19},{4,20},{5,21},{6,22},{7,23},{8,24},{9,... | collective-permute-start | bytes 589832 | tf_op jit(solution)/shard_map/ppermute | solution.py:33
  23.6 12.1 %collective-permute-start.2 = (bf16[128,768]{1,0:T(8,128)(2,1)S(1)}, bf16[128,768]{1,0:T(8,128)(2,1)S(1)}, u32[]{:S(2)}, u32[]{:S(2)}) collective-permute-start(bf16[128,768]{1,0:T(8,128)(2,1)S(1)} %get-tuple-element.39), channel_id=1, source_target_pairs={{0,32},{1,33},{2,34},{3,35},{4,36},{5,37},{6,38},{7,39},{8,40},{9,... | collective-permute-start | bytes 589832 | tf_op jit(solution)/shard_map/ppermute | solution.py:33
  26.5 11.8 %collective-permute-start.3 = (bf16[128,768]{1,0:T(8,128)(2,1)S(1)}, bf16[128,768]{1,0:T(8,128)(2,1)S(1)}, u32[]{:S(2)}, u32[]{:S(2)}) collective-permute-start(bf16[128,768]{1,0:T(8,128)(2,1)S(1)} %get-tuple-element.38.after), channel_id=1, source_target_pairs={{0,48},{1,49},{2,50},{3,51},{4,52},{5,53},{6,54},{7,55},{8,56},{9,... | collective-permute-start | bytes 589832 | tf_op jit(solution)/shard_map/ppermute | solution.py:33
  38.3 11.4 %collective-permute-start.4 = (bf16[32,768]{1,0:T(8,128)(2,1)S(1)}, bf16[32,768]{1,0:T(8,128)(2,1)S(1)}, u32[]{:S(2)}, u32[]{:S(2)}) collective-permute-start(bf16[32,768]{1,0:T(8,128)(2,1)S(1)} %get-tuple-element.43), channel_id=1, source_target_pairs={{0,4},{1,5},{2,6},{3,7},{4,0},{5,1},{6,2},{7,3},{8,12},{9,13},{10,... | collective-permute-start | bytes 147464 | tf_op jit(solution)/shard_map/ppermute | solution.py:33
  40.3 9.4 %collective-permute-start.6 = (bf16[32,768]{1,0:T(8,128)(2,1)S(1)}, bf16[32,768]{1,0:T(8,128)(2,1)S(1)}, u32[]{:S(2)}, u32[]{:S(2)}) collective-permute-start(bf16[32,768]{1,0:T(8,128)(2,1)S(1)} %get-tuple-element.44), channel_id=1, source_target_pairs={{0,12},{1,13},{2,14},{3,15},{4,8},{5,9},{6,10},{7,11},{8,4},{9,5},... | collective-permute-start | bytes 147464 | tf_op jit(solution)/shard_map/ppermute | solution.py:33
  42.4 7.3 %collective-permute-start.5 = (bf16[32,768]{1,0:T(8,128)(2,1)S(1)}, bf16[32,768]{1,0:T(8,128)(2,1)S(1)}, u32[]{:S(2)}, u32[]{:S(2)}) collective-permute-start(bf16[32,768]{1,0:T(8,128)(2,1)S(1)} %get-tuple-element.45), channel_id=1, source_target_pairs={{0,8},{1,9},{2,10},{3,11},{4,12},{5,13},{6,14},{7,15},{8,0},{9,1},... | collective-permute-start | bytes 147464 | tf_op jit(solution)/shard_map/ppermute | solution.py:33
  43.0 2.8 %copy-start.1 = (bf16[6144,512]{1,0:T(8,128)(2,1)S(1)}, bf16[6144,512]{1,0:T(8,128)(2,1)}, u32[]{:S(2)}) copy-start(bf16[6144,512]{1,0:T(8,128)(2,1)} %qkv_ref.1) | copy-start | bytes 18874372
  45.8 2.3 %copy-start.2 = (bf16[384,6144]{1,0:T(8,128)(2,1)S(1)}, bf16[384,6144]{1,0:T(8,128)(2,1)}, u32[]{:S(2)}) copy-start(bf16[384,6144]{1,0:T(8,128)(2,1)} %out_ref.1) | copy-start | bytes 14155780
  48.9 0.8 copy-start.9
  49.8 7.0 %collective-permute-start.9 = (bf16[32,768]{1,0:T(8,128)(2,1)S(1)}, bf16[32,768]{1,0:T(8,128)(2,1)S(1)}, u32[]{:S(2)}, u32[]{:S(2)}) collective-permute-start(bf16[32,768]{1,0:T(8,128)(2,1)S(1)} %fusion.30.a), channel_id=1, source_target_pairs={{0,66},{1,67},{2,64},{3,65},{4,70},{5,71},{6,68},{7,69},{8,74},{9,... | collective-permute-start | bytes 147464 | tf_op jit(solution)/shard_map/ppermute | solution.py:33
  52.5 5.6 %collective-permute-start.8 = (bf16[32,768]{1,0:T(8,128)(2,1)S(1)}, bf16[32,768]{1,0:T(8,128)(2,1)S(1)}, u32[]{:S(2)}, u32[]{:S(2)}) collective-permute-start(bf16[32,768]{1,0:T(8,128)(2,1)S(1)} %fusion.30.a), channel_id=1, source_target_pairs={{0,2},{1,3},{2,0},{3,1},{4,6},{5,7},{6,4},{7,5},{8,10},{9,11},{10,... | collective-permute-start | bytes 147464 | tf_op jit(solution)/shard_map/ppermute | solution.py:33
  52.9 5.2 %collective-permute-start.7 = (bf16[32,768]{1,0:T(8,128)(2,1)S(1)}, bf16[32,768]{1,0:T(8,128)(2,1)S(1)}, u32[]{:S(2)}, u32[]{:S(2)}) collective-permute-start(bf16[32,768]{1,0:T(8,128)(2,1)S(1)} %fusion.30.a), channel_id=1, source_target_pairs={{0,64},{1,65},{2,66},{3,67},{4,68},{5,69},{6,70},{7,71},{8,72},{9,... | collective-permute-start | bytes 147464 | tf_op jit(solution)/shard_map/ppermute | solution.py:33
  58.3 6.6 %collective-permute-start.12 = (bf16[32,768]{1,0:T(8,128)(2,1)S(1)}, bf16[32,768]{1,0:T(8,128)(2,1)S(1)}, u32[]{:S(2)}, u32[]{:S(2)}) collective-permute-start(bf16[32,768]{1,0:T(8,128)(2,1)S(1)} %settle.1.refs_0_), channel_id=1, source_target_pairs={{0,12},{1,13},{2,14},{3,15},{4,8},{5,9},{6,10},{7,11},{8,4},{9,5},... | collective-permute-start | bytes 147464 | tf_op jit(solution)/shard_map/ppermute | solution.py:33
  61.0 5.6 %collective-permute-start.11 = (bf16[32,768]{1,0:T(8,128)(2,1)S(1)}, bf16[32,768]{1,0:T(8,128)(2,1)S(1)}, u32[]{:S(2)}, u32[]{:S(2)}) collective-permute-start(bf16[32,768]{1,0:T(8,128)(2,1)S(1)} %settle.1.refs_0_), channel_id=1, source_target_pairs={{0,8},{1,9},{2,10},{3,11},{4,12},{5,13},{6,14},{7,15},{8,0},{9,1},... | collective-permute-start | bytes 147464 | tf_op jit(solution)/shard_map/ppermute | solution.py:33
  61.9 4.7 %collective-permute-start.10 = (bf16[32,768]{1,0:T(8,128)(2,1)S(1)}, bf16[32,768]{1,0:T(8,128)(2,1)S(1)}, u32[]{:S(2)}, u32[]{:S(2)}) collective-permute-start(bf16[32,768]{1,0:T(8,128)(2,1)S(1)} %settle.1.refs_0_), channel_id=1, source_target_pairs={{0,4},{1,5},{2,6},{3,7},{4,0},{5,1},{6,2},{7,3},{8,12},{9,13},{10,... | collective-permute-start | bytes 147464 | tf_op jit(solution)/shard_map/ppermute | solution.py:33
  66.6 9.1 %collective-permute-start.18 = (bf16[128,768]{1,0:T(8,128)(2,1)S(1)}, bf16[128,768]{1,0:T(8,128)(2,1)S(1)}, u32[]{:S(2)}, u32[]{:S(2)}) collective-permute-start(bf16[128,768]{1,0:T(8,128)(2,1)S(1)} %stack.33.p0), channel_id=1, source_target_pairs={{0,48},{1,49},{2,50},{3,51},{4,52},{5,53},{6,54},{7,55},{8,56},{9,... | collective-permute-start | bytes 589832 | tf_op jit(solution)/shard_map/ppermute | solution.py:33
  67.0 8.7 %collective-permute-start.16 = (bf16[128,768]{1,0:T(8,128)(2,1)S(1)}, bf16[128,768]{1,0:T(8,128)(2,1)S(1)}, u32[]{:S(2)}, u32[]{:S(2)}) collective-permute-start(bf16[128,768]{1,0:T(8,128)(2,1)S(1)} %stack.33.p0), channel_id=1, source_target_pairs={{0,32},{1,33},{2,34},{3,35},{4,36},{5,37},{6,38},{7,39},{8,40},{9,... | collective-permute-start | bytes 589832 | tf_op jit(solution)/shard_map/ppermute | solution.py:33
  67.7 8.8 %collective-permute-start.14 = (bf16[128,768]{1,0:T(8,128)(2,1)S(1)}, bf16[128,768]{1,0:T(8,128)(2,1)S(1)}, u32[]{:S(2)}, u32[]{:S(2)}) collective-permute-start(bf16[128,768]{1,0:T(8,128)(2,1)S(1)} %stack.33.p0), channel_id=1, source_target_pairs={{0,16},{1,17},{2,18},{3,19},{4,20},{5,21},{6,22},{7,23},{8,24},{9,... | collective-permute-start | bytes 589832 | tf_op jit(solution)/shard_map/ppermute | solution.py:33
  70.8 7.6 %collective-permute-start.13 = (bf16[128,768]{1,0:T(8,128)(2,1)S(1)}, bf16[128,768]{1,0:T(8,128)(2,1)S(1)}, u32[]{:S(2)}, u32[]{:S(2)}) collective-permute-start(bf16[128,768]{1,0:T(8,128)(2,1)S(1)} %stack.33.p0), channel_id=1, source_target_pairs={{0,1},{1,0},{2,3},{3,2},{4,5},{5,4},{6,7},{7,6},{8,9},{9,8},{10,11... | collective-permute-start | bytes 589832 | tf_op jit(solution)/shard_map/ppermute | solution.py:33
  75.7 2.7 %collective-permute-start.19 = (bf16[128,768]{1,0:T(8,128)(2,1)S(1)}, bf16[128,768]{1,0:T(8,128)(2,1)S(1)}, u32[]{:S(2)}, u32[]{:S(2)}) collective-permute-start(bf16[128,768]{1,0:T(8,128)(2,1)S(1)} %collective-permute-done.18.p3), channel_id=1, source_target_pairs={{0,1},{1,0},{2,3},{3,2},{4,5},{5,4},{6,7},{7,6},{8,9},{9,8},{10,11... | collective-permute-start | bytes 589832 | tf_op jit(solution)/shard_map/ppermute | solution.py:33
  75.7 2.7 %collective-permute-start.17 = (bf16[128,768]{1,0:T(8,128)(2,1)S(1)}, bf16[128,768]{1,0:T(8,128)(2,1)S(1)}, u32[]{:S(2)}, u32[]{:S(2)}) collective-permute-start(bf16[128,768]{1,0:T(8,128)(2,1)S(1)} %collective-permute-done.16.p2), channel_id=1, source_target_pairs={{0,1},{1,0},{2,3},{3,2},{4,5},{5,4},{6,7},{7,6},{8,9},{9,8},{10,11... | collective-permute-start | bytes 589832 | tf_op jit(solution)/shard_map/ppermute | solution.py:33
  76.6 1.9 %collective-permute-start.15 = (bf16[128,768]{1,0:T(8,128)(2,1)S(1)}, bf16[128,768]{1,0:T(8,128)(2,1)S(1)}, u32[]{:S(2)}, u32[]{:S(2)}) collective-permute-start(bf16[128,768]{1,0:T(8,128)(2,1)S(1)} %collective-permute-done.14.p1), channel_id=1, source_target_pairs={{0,1},{1,0},{2,3},{3,2},{4,5},{5,4},{6,7},{7,6},{8,9},{9,8},{10,11... | collective-permute-start | bytes 589832 | tf_op jit(solution)/shard_map/ppermute | solution.py:33
  78.4 13.4 %copy-start.3 = (bf16[1,2,4096,256]{3,2,1,0:T(8,128)(2,1)S(1)}, bf16[1,2,4096,256]{3,2,1,0:T(8,128)(2,1)}, u32[]{:S(2)}) copy-start(bf16[1,2,4096,256]{3,2,1,0:T(8,128)(2,1)} %cache.1) | copy-start | bytes 12582916
  78.4 13.4 %copy-start.7 = (s32[4]{0:T(128)S(1)}, s32[4]{0:T(128)}, u32[]{:S(2)}) copy-start(s32[4]{0:T(128)} %lengths.1) | copy-start | bytes 52
  78.4 13.4 %copy-start.8 = (f32[1,128]{1,0:T(1,128)S(1)}, f32[1,128]{1,0:T(1,128)}, u32[]{:S(2)}) copy-start(f32[1,128]{1,0:T(1,128)} %constant.68.clone.freq_ref) | copy-start | bytes 1540
  80.3 15.8 %copy-start.10 = (bf16[48,6144]{1,0:T(8,128)(2,1)S(1)}, bf16[48,6144]{1,0:T(8,128)(2,1)}, u32[]{:S(2)}) copy-start(bf16[48,6144]{1,0:T(8,128)(2,1)} %copy-done.9) | copy-start | bytes 1769476
  80.3 4.8 %collective-permute-start.20 = (bf16[32,512]{1,0:T(8,128)(2,1)S(1)}, bf16[32,512]{1,0:T(8,128)(2,1)S(1)}, u32[]{:S(2)}, u32[]{:S(2)}) collective-permute-start(bf16[32,512]{1,0:T(8,128)(2,1)S(1)} %get-tuple-element.23), channel_id=1, source_target_pairs={{0,16},{1,17},{2,18},{3,19},{4,20},{5,21},{6,22},{7,23},{8,24},{9,... | collective-permute-start | bytes 98312 | tf_op jit(solution)/shard_map/ppermute | solution.py:33
  80.4 5.5 %collective-permute-start.21 = (bf16[32,512]{1,0:T(8,128)(2,1)S(1)}, bf16[32,512]{1,0:T(8,128)(2,1)S(1)}, u32[]{:S(2)}, u32[]{:S(2)}) collective-permute-start(bf16[32,512]{1,0:T(8,128)(2,1)S(1)} %get-tuple-element.24), channel_id=1, source_target_pairs={{0,32},{1,33},{2,34},{3,35},{4,36},{5,37},{6,38},{7,39},{8,40},{9,... | collective-permute-start | bytes 98312 | tf_op jit(solution)/shard_map/ppermute | solution.py:33
  82.9 5.1 %collective-permute-start.22 = (bf16[32,512]{1,0:T(8,128)(2,1)S(1)}, bf16[32,512]{1,0:T(8,128)(2,1)S(1)}, u32[]{:S(2)}, u32[]{:S(2)}) collective-permute-start(bf16[32,512]{1,0:T(8,128)(2,1)S(1)} %get-tuple-element.25), channel_id=1, source_target_pairs={{0,48},{1,49},{2,50},{3,51},{4,52},{5,53},{6,54},{7,55},{8,56},{9,... | collective-permute-start | bytes 98312 | tf_op jit(solution)/shard_map/ppermute | solution.py:33
  88.1 3.7 %collective-permute-start.23 = (bf16[8,512]{1,0:T(8,128)(2,1)S(1)}, bf16[8,512]{1,0:T(8,128)(2,1)S(1)}, u32[]{:S(2)}, u32[]{:S(2)}) collective-permute-start(bf16[8,512]{1,0:T(8,128)(2,1)S(1)} %get-tuple-element.27), channel_id=1, source_target_pairs={{0,64},{1,65},{2,66},{3,67},{4,68},{5,69},{6,70},{7,71},{8,72},{9,... | collective-permute-start | bytes 24584 | tf_op jit(solution)/shard_map/ppermute | solution.py:33
  88.4 3.4 %collective-permute-start.24 = (bf16[8,512]{1,0:T(8,128)(2,1)S(1)}, bf16[8,512]{1,0:T(8,128)(2,1)S(1)}, u32[]{:S(2)}, u32[]{:S(2)}) collective-permute-start(bf16[8,512]{1,0:T(8,128)(2,1)S(1)} %get-tuple-element.28), channel_id=1, source_target_pairs={{0,1},{1,0},{2,3},{3,2},{4,5},{5,4},{6,7},{7,6},{8,9},{9,8},{10,11... | collective-permute-start | bytes 24584 | tf_op jit(solution)/shard_map/ppermute | solution.py:33
  88.4 3.4 %collective-permute-start.25 = (bf16[8,512]{1,0:T(8,128)(2,1)S(1)}, bf16[8,512]{1,0:T(8,128)(2,1)S(1)}, u32[]{:S(2)}, u32[]{:S(2)}) collective-permute-start(bf16[8,512]{1,0:T(8,128)(2,1)S(1)} %get-tuple-element.29), channel_id=1, source_target_pairs={{0,65},{1,64},{2,67},{3,66},{4,69},{5,68},{6,71},{7,70},{8,73},{9,... | collective-permute-start | bytes 24584 | tf_op jit(solution)/shard_map/ppermute | solution.py:33
  93.9 5.8 %collective-permute-start.28 = (bf16[8,384]{1,0:T(8,128)(2,1)S(1)}, bf16[8,384]{1,0:T(8,128)(2,1)S(1)}, u32[]{:S(2)}, u32[]{:S(2)}) collective-permute-start(bf16[8,384]{1,0:T(8,128)(2,1)S(1)} %get-tuple-element.31), channel_id=1, source_target_pairs={{0,65},{1,64},{2,67},{3,66},{4,69},{5,68},{6,71},{7,70},{8,73},{9,... | collective-permute-start | bytes 18440 | tf_op jit(solution)/shard_map/ppermute | solution.py:33
  95.5 4.2 %collective-permute-start.26 = (bf16[8,384]{1,0:T(8,128)(2,1)S(1)}, bf16[8,384]{1,0:T(8,128)(2,1)S(1)}, u32[]{:S(2)}, u32[]{:S(2)}) collective-permute-start(bf16[8,384]{1,0:T(8,128)(2,1)S(1)} %get-tuple-element.31), channel_id=1, source_target_pairs={{0,1},{1,0},{2,3},{3,2},{4,5},{5,4},{6,7},{7,6},{8,9},{9,8},{10,11... | collective-permute-start | bytes 18440 | tf_op jit(solution)/shard_map/ppermute | solution.py:33
  95.5 4.1 %collective-permute-start.27 = (bf16[8,384]{1,0:T(8,128)(2,1)S(1)}, bf16[8,384]{1,0:T(8,128)(2,1)S(1)}, u32[]{:S(2)}, u32[]{:S(2)}) collective-permute-start(bf16[8,384]{1,0:T(8,128)(2,1)S(1)} %get-tuple-element.30.keep0), channel_id=1, source_target_pairs={{0,64},{1,65},{2,66},{3,67},{4,68},{5,69},{6,70},{7,71},{8,72},{9,... | collective-permute-start | bytes 18440 | tf_op jit(solution)/shard_map/ppermute | solution.py:33
  100.2 5.1 %collective-permute-start.31 = (bf16[32,384]{1,0:T(8,128)(2,1)S(1)}, bf16[32,384]{1,0:T(8,128)(2,1)S(1)}, u32[]{:S(2)}, u32[]{:S(2)}) collective-permute-start(bf16[32,384]{1,0:T(8,128)(2,1)S(1)} %heads.1.a0), channel_id=1, source_target_pairs={{0,48},{1,49},{2,50},{3,51},{4,52},{5,53},{6,54},{7,55},{8,56},{9,... | collective-permute-start | bytes 73736 | tf_op jit(solution)/shard_map/ppermute | solution.py:33
  102.5 5.3 %collective-permute-start.30 = (bf16[32,384]{1,0:T(8,128)(2,1)S(1)}, bf16[32,384]{1,0:T(8,128)(2,1)S(1)}, u32[]{:S(2)}, u32[]{:S(2)}) collective-permute-start(bf16[32,384]{1,0:T(8,128)(2,1)S(1)} %heads.1.a0), channel_id=1, source_target_pairs={{0,32},{1,33},{2,34},{3,35},{4,36},{5,37},{6,38},{7,39},{8,40},{9,... | collective-permute-start | bytes 73736 | tf_op jit(solution)/shard_map/ppermute | solution.py:33
  102.5 5.3 %collective-permute-start.29 = (bf16[32,384]{1,0:T(8,128)(2,1)S(1)}, bf16[32,384]{1,0:T(8,128)(2,1)S(1)}, u32[]{:S(2)}, u32[]{:S(2)}) collective-permute-start(bf16[32,384]{1,0:T(8,128)(2,1)S(1)} %heads.1.a0), channel_id=1, source_target_pairs={{0,16},{1,17},{2,18},{3,19},{4,20},{5,21},{6,22},{7,23},{8,24},{9,... | collective-permute-start | bytes 73736 | tf_op jit(solution)/shard_map/ppermute | solution.py:33
  110.6 3.1 %collective-permute-start.32 = (bf16[4,4,2,32,384]{4,3,2,1,0:T(8,128)(2,1)S(1)}, bf16[4,4,2,32,384]{4,3,2,1,0:T(8,128)(2,1)S(1)}, u32[]{:S(2)}, u32[]{:S(2)}) collective-permute-start(bf16[4,4,2,32,384]{4,3,2,1,0:T(8,128)(2,1)S(1)} %share.3), channel_id=1, source_target_pairs={{0,1},{1,0},{2,3},{3,2},{4,5},{5,4},{6,7},{7,6},{8,9},{9,8},{10,11... | collective-permute-start | bytes 2359304 | tf_op jit(solution)/shard_map/ppermute | solution.py:33
  114.0 12.8 %collective-permute-start.35 = (bf16[4,2,32,384]{3,2,1,0:T(8,128)(2,1)S(1)}, bf16[4,2,32,384]{3,2,1,0:T(8,128)(2,1)S(1)}, u32[]{:S(2)}, u32[]{:S(2)}) collective-permute-start(bf16[4,2,32,384]{3,2,1,0:T(8,128)(2,1)S(1)} %get-tuple-element.34), channel_id=1, source_target_pairs={{0,12},{1,13},{2,14},{3,15},{4,8},{5,9},{6,10},{7,11},{8,4},{9,5},... | collective-permute-start | bytes 589832 | tf_op jit(solution)/shard_map/ppermute | solution.py:33
  115.5 11.3 %collective-permute-start.34 = (bf16[4,2,32,384]{3,2,1,0:T(8,128)(2,1)S(1)}, bf16[4,2,32,384]{3,2,1,0:T(8,128)(2,1)S(1)}, u32[]{:S(2)}, u32[]{:S(2)}) collective-permute-start(bf16[4,2,32,384]{3,2,1,0:T(8,128)(2,1)S(1)} %get-tuple-element.35), channel_id=1, source_target_pairs={{0,8},{1,9},{2,10},{3,11},{4,12},{5,13},{6,14},{7,15},{8,0},{9,1},... | collective-permute-start | bytes 589832 | tf_op jit(solution)/shard_map/ppermute | solution.py:33
  116.4 11.0 %collective-permute-start.33 = (bf16[4,2,32,384]{3,2,1,0:T(8,128)(2,1)S(1)}, bf16[4,2,32,384]{3,2,1,0:T(8,128)(2,1)S(1)}, u32[]{:S(2)}, u32[]{:S(2)}) collective-permute-start(bf16[4,2,32,384]{3,2,1,0:T(8,128)(2,1)S(1)} %get-tuple-element.36), channel_id=1, source_target_pairs={{0,4},{1,5},{2,6},{3,7},{4,0},{5,1},{6,2},{7,3},{8,12},{9,13},{10,... | collective-permute-start | bytes 589832 | tf_op jit(solution)/shard_map/ppermute | solution.py:33
  127.5 4.4 %collective-permute-start.36 = (bf16[2,32,384]{2,1,0:T(8,128)(2,1)S(1)}, bf16[2,32,384]{2,1,0:T(8,128)(2,1)S(1)}, u32[]{:S(2)}, u32[]{:S(2)}) collective-permute-start(bf16[2,32,384]{2,1,0:T(8,128)(2,1)S(1)} %get-tuple-element.40), channel_id=1, source_target_pairs={{0,16},{1,17},{2,18},{3,19},{4,20},{5,21},{6,22},{7,23},{8,24},{9,... | collective-permute-start | bytes 147464 | tf_op jit(solution)/shard_map/ppermute | solution.py:33
  128.0 5.8 %collective-permute-start.38 = (bf16[2,32,384]{2,1,0:T(8,128)(2,1)S(1)}, bf16[2,32,384]{2,1,0:T(8,128)(2,1)S(1)}, u32[]{:S(2)}, u32[]{:S(2)}) collective-permute-start(bf16[2,32,384]{2,1,0:T(8,128)(2,1)S(1)} %get-tuple-element.41), channel_id=1, source_target_pairs={{0,48},{1,49},{2,50},{3,51},{4,52},{5,53},{6,54},{7,55},{8,56},{9,... | collective-permute-start | bytes 147464 | tf_op jit(solution)/shard_map/ppermute | solution.py:33
  130.2 5.6 %collective-permute-start.37 = (bf16[2,32,384]{2,1,0:T(8,128)(2,1)S(1)}, bf16[2,32,384]{2,1,0:T(8,128)(2,1)S(1)}, u32[]{:S(2)}, u32[]{:S(2)}) collective-permute-start(bf16[2,32,384]{2,1,0:T(8,128)(2,1)S(1)} %get-tuple-element.42), channel_id=1, source_target_pairs={{0,32},{1,33},{2,34},{3,35},{4,36},{5,37},{6,38},{7,39},{8,40},{9,... | collective-permute-start | bytes 147464 | tf_op jit(solution)/shard_map/ppermute | solution.py:33
  135.8 5.0 %collective-permute-start.41 = (bf16[16,384]{1,0:T(8,128)(2,1)S(1)}, bf16[16,384]{1,0:T(8,128)(2,1)S(1)}, u32[]{:S(2)}, u32[]{:S(2)}) collective-permute-start(bf16[16,384]{1,0:T(8,128)(2,1)S(1)} %get-tuple-element.46), channel_id=1, source_target_pairs={{0,66},{1,67},{2,64},{3,65},{4,70},{5,71},{6,68},{7,69},{8,74},{9,... | collective-permute-start | bytes 36872 | tf_op jit(solution)/shard_map/ppermute | solution.py:33
  137.9 5.2 %collective-permute-start.40 = (bf16[16,384]{1,0:T(8,128)(2,1)S(1)}, bf16[16,384]{1,0:T(8,128)(2,1)S(1)}, u32[]{:S(2)}, u32[]{:S(2)}) collective-permute-start(bf16[16,384]{1,0:T(8,128)(2,1)S(1)} %get-tuple-element.47), channel_id=1, source_target_pairs={{0,2},{1,3},{2,0},{3,1},{4,6},{5,7},{6,4},{7,5},{8,10},{9,11},{10,... | collective-permute-start | bytes 36872 | tf_op jit(solution)/shard_map/ppermute | solution.py:33
  139.4 3.7 %collective-permute-start.39 = (bf16[16,384]{1,0:T(8,128)(2,1)S(1)}, bf16[16,384]{1,0:T(8,128)(2,1)S(1)}, u32[]{:S(2)}, u32[]{:S(2)}) collective-permute-start(bf16[16,384]{1,0:T(8,128)(2,1)S(1)} %get-tuple-element.48), channel_id=1, source_target_pairs={{0,64},{1,65},{2,66},{3,67},{4,68},{5,69},{6,70},{7,71},{8,72},{9,... | collective-permute-start | bytes 36872 | tf_op jit(solution)/shard_map/ppermute | solution.py:33
